TPU v7x, 256 devices: a whole 4x4x8 slice. The times are simulated.
256 devices in a mesh: expert: 64 (over y_lo, x, z), tensor: 4 (over y_hi, core).
Axes of the slice: x: 4, y: 4 (y_hi: 2, y_lo: 2; y = y_hi * 2 + y_lo), z: 8, core: 2. Of those that a mesh axis runs over, the one named last changes fastest.
Arguments:
- tokens: bfloat16 [4096, 2, 2880], P('expert', None, 'tensor'), may hold values from -40 to 40
- attn_gain: float32 [2880], replicated, may hold values from 0.25 to 1.75
- w_query: bfloat16 [2880, 2048], P(None, 'tensor'), may hold values from -0.109375 to 0.109375
- key_value_weight: bfloat16 [2880, 4, 128], P(None, 'tensor'), may hold values from -0.625 to 0.625
- w_out: bfloat16 [2048, 2880], P('tensor'), may hold values from -0.125 to 0.125
- cache_keyval: bfloat16 [12288, 2, 4, 128], P('expert', None, 'tensor'), may hold values from -130 to 130
- prefix_length: int32 [2], replicated, may hold values from 3072 to 12288, as said below
- routed_experts: int32 [4096, 2, 4], P('expert'), may hold values from 0 to 63, all different within a row; in each aligned block of 128 rows (0 to 127, 128 to 255, ..., all dimensions but the last counted through in order) at most 20 rows name the same one
- route_weights: float32 [4096, 2, 4], P('expert'), may hold values from 0.1 to 0.6
- expert_gain: float32 [2880], replicated, may hold values from 0.25 to 1.75
- w_gate_up: bfloat16 [64, 2880, 2, 1440], P('expert', None, None, 'tensor'), may hold values from -0.109375 to 0.109375
- w_down: bfloat16 [64, 1440, 2880], P('expert', 'tensor'), may hold values from -0.15625 to 0.15625
Outputs:
- layer_output: bfloat16 [4096, 2, 2880], P('expert', None, 'tensor')
- new_key_value_rows: bfloat16 [4096, 2, 4, 128], P('expert', None, 'tensor')
Inputs may be any that keep to these rules, and one draw needn't show every extreme that they name: `prefix_length`: one sequence, drawn from the seed, has a full cache of 12288 positions; no sequence has fewer than 3072. `routed_experts`: each token names 4 different experts. Taking tokens in position-major order, in each aligned block of 128 tokens (the tokens of one index of expert) at most 20 name the same expert, and in some blocks one expert is named by exactly 20.
All inputs are finite; a program needn't handle non-finite values.
Results may differ from a plain program's by a relative error of at most 0.02.
Values may be sent and summed in bfloat16 or wider, within the bound.
A program may use at most 128 MiB of HBM per device.

v0:
```python
import math

import jax
import jax.numpy as jnp
from jax import lax
from jax.sharding import PartitionSpec as P

EPSILON = 1e-05
ROPE_BASE = 150000.0


def rotate(vectors, places):
    half_dim = vectors.shape[-1] // 2
    steps_up = jnp.arange(half_dim, dtype=jnp.float32)
    frequency = jnp.exp(steps_up * (-math.log(ROPE_BASE) / half_dim))
    angles = places[..., None] * frequency
    cosine = jnp.cos(angles)
    sine_part = jnp.sin(angles)
    first_half = vectors[..., :half_dim]
    second_half = vectors[..., half_dim:]
    return jnp.concatenate(
        [
            first_half * cosine - second_half * sine_part,
            second_half * cosine + first_half * sine_part,
        ],
        axis=-1,
    )


def on_device(
    tokens,
    attn_gain,
    w_query,
    key_value_weight,
    w_out,
    cache_keyval,
    prefix_length,
    routed_experts,
    route_weights,
    expert_gain,
    w_gate_up,
    w_down,
):
    span_dev, seq_count, quarter = tokens.shape
    model_width = attn_gain.shape[0]
    row_count = span_dev * seq_count
    local_kv = key_value_weight.shape[1]
    head_dim = key_value_weight.shape[2] // 2
    query_cols = w_query.shape[1]
    group_width = query_cols // head_dim // local_kv
    cache_rows = cache_keyval.shape[0]
    tensor_rank = lax.axis_index("tensor")
    expert_rank = lax.axis_index("expert")
    shard_piece = lax.all_gather(tokens, "tensor", axis=2, tiled=True)
    col_count = shard_piece.shape[2]
    piece_rows = shard_piece.reshape(row_count, col_count).astype(jnp.float32)
    rescaled = (piece_rows * attn_gain).astype(jnp.bfloat16)
    keyval_rows = key_value_weight.reshape(col_count, local_kv * 2 * head_dim)
    query_acc = jnp.dot(rescaled, w_query, preferred_element_type=jnp.float32)
    keyval_acc = jnp.dot(rescaled, keyval_rows, preferred_element_type=jnp.float32)
    square_sum = jnp.sum(piece_rows * piece_rows, axis=1)
    inverse_square_root = lax.rsqrt(square_sum / model_width + EPSILON)
    span_place = expert_rank * span_dev + jnp.arange(span_dev, dtype=jnp.int32)
    places = (prefix_length[None, :] + span_place[:, None]).reshape(row_count).astype(jnp.float32)
    query_matrix = rotate(
        (query_acc * inverse_square_root[:, None]).reshape(
            row_count, query_cols // head_dim, head_dim
        ),
        places[:, None],
    ).astype(jnp.bfloat16)
    key_value_heads = (keyval_acc * inverse_square_root[:, None]).reshape(
        row_count, local_kv, 2 * head_dim
    )
    rotated_keys = rotate(key_value_heads[..., :head_dim], places[:, None])
    new_key_value_rows = jnp.concatenate(
        [rotated_keys, key_value_heads[..., head_dim:]], axis=-1
    ).astype(jnp.bfloat16)
    new_key_value_rows = new_key_value_rows.reshape(span_dev, seq_count, local_kv, 2 * head_dim)
    query_count = span_dev * group_width
    query_heads = query_matrix.reshape(
        span_dev, seq_count, local_kv, group_width, head_dim
    ).transpose(1, 2, 0, 3, 4)
    query_heads = query_heads.reshape(seq_count, local_kv, query_count, head_dim)
    query_place = expert_rank * span_dev + jnp.arange(query_count, dtype=jnp.int32) // group_width
    stride = cache_rows + span_dev
    score_scale = head_dim ** (-0.5)
    joined = jnp.concatenate([cache_keyval, new_key_value_rows], axis=0)
    start_state = (
        jnp.full((seq_count, local_kv, query_count), -1e30, jnp.float32),
        jnp.zeros((seq_count, local_kv, query_count), jnp.float32),
        jnp.zeros((seq_count, local_kv, query_count, head_dim), jnp.float32),
    )
    key_piece = lax.all_gather(joined, "expert", axis=0, tiled=True)
    key_count = key_piece.shape[0]
    block_size = math.gcd(key_count, 2048)

    def one_block(loop_index, running):
        running_max, running_sum, running_out = running
        key_block = lax.dynamic_slice_in_dim(key_piece, loop_index * block_size, block_size, 0)
        global_row = loop_index * block_size + jnp.arange(block_size, dtype=jnp.int32)
        source_dev = global_row // stride
        offset = global_row % stride
        in_cache = offset < cache_rows
        cache_place = source_dev * cache_rows + offset
        key_place = source_dev * span_dev + offset - cache_rows
        scores = (
            jnp.einsum(
                "shqd,kshd->shqk",
                query_heads,
                key_block[..., :head_dim],
                preferred_element_type=jnp.float32,
            )
            * score_scale
        )
        cache_ok = cache_place[None, :] < prefix_length[:, None]
        span_ok = key_place[None, :] <= query_place[:, None]
        allowed = jnp.where(
            in_cache[None, None, None, :], cache_ok[:, None, None, :], span_ok[None, None, :, :]
        )
        masked = jnp.where(allowed, scores, -1e30)
        next_max = jnp.maximum(running_max, jnp.max(masked, axis=-1))
        weights = jnp.where(allowed, jnp.exp(masked - next_max[..., None]), 0.0)
        shrink_factor = jnp.exp(running_max - next_max)
        next_sum = running_sum * shrink_factor + jnp.sum(weights, axis=-1)
        next_out = running_out * shrink_factor[..., None] + jnp.einsum(
            "shqk,kshd->shqd",
            weights.astype(jnp.bfloat16),
            key_block[..., head_dim:],
            preferred_element_type=jnp.float32,
        )
        return (next_max, next_sum, next_out)

    final_max, final_sum, final_out = lax.fori_loop(
        0, key_count // block_size, one_block, start_state
    )
    attended = (final_out / final_sum[..., None]).astype(jnp.bfloat16)
    attended = (
        attended.reshape(seq_count, local_kv, span_dev, group_width, head_dim)
        .transpose(2, 0, 1, 3, 4)
        .reshape(row_count, query_cols)
    )
    projected = jnp.dot(attended, w_out, preferred_element_type=jnp.float32)
    own_cols = lax.dynamic_slice_in_dim(
        projected, tensor_rank * quarter, quarter, 1
    ) + tokens.reshape(row_count, quarter).astype(jnp.float32)
    residual_term = lax.dynamic_update_slice_in_dim(projected, own_cols, tensor_rank * quarter, 1)
    hidden_sum = lax.psum(residual_term.astype(jnp.bfloat16), "tensor")
    hidden_wide = lax.optimization_barrier(hidden_sum).astype(jnp.float32)
    second_root = lax.rsqrt(jnp.sum(hidden_wide * hidden_wide, axis=1) / model_width + EPSILON)
    normed = (hidden_wide * second_root[:, None] * expert_gain).astype(jnp.bfloat16)
    top_count = routed_experts.shape[2]
    expert_count = lax.axis_size("expert")
    capacity = min(row_count, max(2, 5 * row_count * top_count // (2 * expert_count)))
    expert_list = routed_experts.reshape(row_count * top_count)
    one_hot = (expert_list[:, None] == jnp.arange(expert_count, dtype=jnp.int32)[None, :]).astype(
        jnp.int32
    )
    earlier = jnp.cumsum(one_hot, axis=0) - one_hot
    arrival = jnp.sum(earlier * one_hot, axis=1)
    slot_index = expert_list * capacity + arrival
    ffn_local = w_down.shape[1]
    gate_up_rows = w_gate_up[0].reshape(model_width, 2 * ffn_local)
    outgoing = (
        jnp.zeros((expert_count * capacity, model_width), jnp.bfloat16)
        .at[slot_index]
        .set(jnp.repeat(normed, top_count, axis=0))
    )
    received = lax.all_to_all(
        outgoing.reshape(expert_count, capacity, model_width),
        "expert",
        split_axis=0,
        concat_axis=0,
        tiled=True,
    )
    gate_up = jnp.dot(
        received.reshape(expert_count * capacity, model_width),
        gate_up_rows,
        preferred_element_type=jnp.float32,
    )
    gate_part = gate_up[:, :ffn_local]
    up_part = gate_up[:, ffn_local:]
    activated = (gate_part * jax.nn.sigmoid(1.702 * gate_part) * (up_part + 1.0)).astype(
        jnp.bfloat16
    )
    partial_value = jnp.dot(activated, w_down[0], preferred_element_type=jnp.float32)
    weight_cols = route_weights.reshape(row_count, top_count, 1)
    owner_sums = lax.psum_scatter(
        partial_value.astype(jnp.bfloat16), "tensor", scatter_dimension=1, tiled=True
    ).astype(jnp.float32)
    returned_rows = lax.all_to_all(
        owner_sums.reshape(expert_count, capacity, quarter).astype(jnp.bfloat16),
        "expert",
        split_axis=0,
        concat_axis=0,
        tiled=True,
    ).astype(jnp.float32)
    picked = returned_rows.reshape(expert_count * capacity, quarter)[slot_index]
    expert_mix = jnp.sum(picked.reshape(row_count, top_count, quarter) * weight_cols, axis=1)
    hidden_quarter = lax.dynamic_slice_in_dim(hidden_wide, tensor_rank * quarter, quarter, 1)
    layer_output = (
        (hidden_quarter + expert_mix).astype(jnp.bfloat16).reshape(span_dev, seq_count, quarter)
    )
    return (layer_output, new_key_value_rows)


def solution(mesh):
    return jax.shard_map(
        on_device,
        mesh=mesh,
        in_specs=(
            P("expert", None, "tensor"),
            P(),
            P(None, "tensor"),
            P(None, "tensor", None),
            P("tensor", None),
            P("expert", None, "tensor", None),
            P(),
            P("expert", None, None),
            P("expert", None, None),
            P(),
            P("expert", None, None, "tensor"),
            P("expert", "tensor", None),
        ),
        out_specs=(P("expert", None, "tensor"), P("expert", None, "tensor", None)),
        check_vma=False,
    )
```

profile of v0, /device:TPU:40, one launch (start us, length us, event | category | flops | bytes accessed | tf_op | source)
XLA Modules:
  0.0 944.3 jit_solution(18429663296265936583)
XLA Ops:
  9.3 13.9 %all_gather.6 = bf16[64,2,2880]{0,1,2:T(2,128)(2,1)} all-gather(bf16[64,2,720]{0,1,2:T(2,128)(2,1)S(1)} %copy.127), channel_id=1, replica_groups=mesh['expert'=64,'tensor'=4] {'tensor'}, dimensions={2}, use_global_device_ids=true | all-gather | bytes 921600 | tf_op jit(solution)/shard_map/all_gather | solution.py:54
  59.6 247.8 %all-gather.2.cloned.1.call-done = bf16[16384,2,1,128]{0,3,1,2:T(8,128)(2,1)} async-done(((bf16[256,2,1,128]{0,3,1,2:T(8,128)(2,1)}), bf16[16384,2,1,128]{0,3,1,2:T(8,128)(2,1)}) %all-gather.2.cloned.1.call-update) | async-done | bytes 8388624 | tf_op jit(solution)/shard_map/all_gather | solution.py:93
  307.4 133.1 %while.20 = (s32[]{:T(128)}, f32[2,1,512]{2,0,1:T(2,128)S(1)}, f32[2,1,512]{2,0,1:T(2,128)S(1)}, f32[2,1,512,64]{2,3,0,1:T(8,128)}, s32[2]{0:T(128)S(1)}, /*inde...) while((s32[]{:T(128)}, f32[2,1,512]{2,0,1:T(2,128)S(1)}, ...), condition=%wide.region_4.5_spmd.clone, body=%wide.region_1.4_spmd.clone.sunk | while | flops 571763200 | bytes 75231592 | solution.py:133
  308.4 6.0 fusion.76
  325.0 6.0 fusion.76
  331.0 5.6 fusion.79
  341.7 6.0 fusion.76
  358.3 6.0 fusion.76
  364.3 5.6 fusion.79
  374.9 6.0 fusion.76
  391.6 6.0 fusion.76
  408.2 6.0 fusion.76
  424.9 6.0 fusion.76
  430.9 5.6 fusion.79
  446.6 45.0 %all-reduce.2.cloned.1.call-done = bf16[128,2880]{0,1:T(8,128)(2,1)} async-done(((bf16[128,2880]{0,1:T(8,128)(2,1)}), bf16[128,2880]{0,1:T(8,128)(2,1)}) %all-reduce.2.cloned.1.call-update) | async-done | bytes 737296 | tf_op jit(solution)/shard_map/psum | solution.py:147
  506.9 10.3 %scatter_custom_fusion = bf16[1280,2880]{1,0:T(8,128)(2,1)} fusion(s32[512]{0:T(512)S(1)} %bitcast.133, bf16[512,2880]{1,0:T(8,128)(2,1)} %reshape.560, bf16[]{:T(256)} %constant.206.clone.1), kind=kCustom, calls=%fused_computation.56 | custom fusion | bytes 7373312 | tf_op jit(solution)/shard_map/scatter | solution.py:166
  517.2 11.4 %reshape.538 = bf16[64,20,2880]{2,1,0:T(8,128)(2,1)} reshape(bf16[1280,2880]{1,0:T(8,128)(2,1)} %scatter_custom_fusion) | data formatting | bytes 14745600 | tf_op jit(solution)/shard_map/reshape | solution.py:169
  528.7 212.9 %all_to_all.10 = bf16[64,20,2880]{2,1,0:T(8,128)(2,1)} all-to-all(bf16[64,20,2880]{2,1,0:T(8,128)(2,1)} %reshape.538), channel_id=1, replica_groups=mesh['expert'=64,'tensor'=4] {'expert'}, dimensions={0} | all-to-all | bytes 14745600 | tf_op jit(solution)/shard_map/all_to_all | solution.py:168
  741.5 12.0 %reshape.539 = bf16[1280,2880]{1,0:T(8,128)(2,1)} reshape(bf16[64,20,2880]{2,1,0:T(8,128)(2,1)} %all_to_all.10) | data formatting | bytes 14745600 | tf_op jit(solution)/shard_map/reshape | solution.py:176
  753.5 10.1 %fusion.60 = f32[1280,720]{0,1:T(8,128)S(1)} fusion(bf16[1280,2880]{1,0:T(8,128)(2,1)} %reshape.539, bf16[2880,720]{0,1:T(8,128)(2,1)} %bitcast.135), kind=kOutput, calls=%fused_computation.118 | convolution fusion | flops 5308416000 | bytes 15206400 | tf_op jit(solution)/shard_map/dot_general | solution.py:175
  763.6 6.8 convolution_convert_fusion
  770.4 72.2 %reduce-scatter.2.cloned.1.call-done = bf16[1280,720]{0,1:T(8,128)(2,1)} async-done(((bf16[1280,2880]{0,1:T(8,128)(2,1)}), bf16[1280,720]{0,1:T(8,128)(2,1)}) %reduce-scatter.2.cloned.1.call-update) | async-done | bytes 1843216 | tf_op jit(solution)/shard_map/reduce_scatter | solution.py:187
  850.6 11.8 %all-to-all-start.1 = ((bf16[64,20,720]{2,1,0:T(8,128)(2,1)}), bf16[64,20,720]{2,1,0:T(8,128)(2,1)}, u32[]{:S(2)}, u32[]{:S(2)}) async-start(bf16[64,20,720]{2,1,0:T(8,128)(2,1)} %convert_element_type.115), calls=%async_computation.2 | async-start | bytes 4718592 | tf_op jit(solution)/shard_map/all_to_all | solution.py:190
  865.6 54.2 %all-to-all-done.1 = bf16[64,20,720]{2,1,0:T(8,128)(2,1)} async-done(((bf16[64,20,720]{2,1,0:T(8,128)(2,1)}), bf16[64,20,720]{2,1,0:T(8,128)(2,1)}, u32[]{:S(2)}, u32[]{:S(2)}) %all-to-all-start.1) | async-done | bytes 1843232 | tf_op jit(solution)/shard_map/all_to_all | solution.py:190
  (284 shorter events, 156.2 us)
Async XLA Ops:
  7.2 435.0 %copy-start = (bf16[512,2880]{0,1:T(8,128)(2,1)S(1)}, bf16[512,2880]{0,1:T(8,128)(2,1)}, u32[]{:S(2)}) copy-start(bf16[512,2880]{0,1:T(8,128)(2,1)} %param.18) | copy-start | bytes 8847364
  7.2 20.2 %copy-start.15 = (f32[2880]{0:T(1024)S(1)}, f32[2880]{0:T(1024)}, u32[]{:S(2)}) copy-start(f32[2880]{0:T(1024)} %param.15) | copy-start | bytes 34564
  7.2 300.2 %all-gather.2.cloned.1.call-start = ((), (), s32[]{:S(2)}) async-start(), calls=%async_computation.3 | async-start | bytes 8519680 | tf_op jit(solution)/shard_map/all_gather | solution.py:93
  7.3 30.4 %copy-start.24 = (f32[32]{0:T(128)}, f32[32]{0:T(128)S(1)}, u32[]{:S(2)}) copy-start(f32[32]{0:T(128)S(1)} %multiply_exponential_fusion) | copy-start | bytes 388
  23.2 12.5 %copy-start.17 = (s32[2]{0:T(128)S(1)}, s32[2]{0:T(128)}, u32[]{:S(2)}) copy-start(s32[2]{0:T(128)} %param.20) | copy-start | bytes 28
  29.7 9.3 copy-start.14
  32.7 10.4 %copy-start.5 = (bf16[64,2,720]{2,1,0:T(2,128)(2,1)S(1)}, bf16[64,2,720]{2,1,0:T(2,128)(2,1)}, u32[]{:S(2)}) copy-start(bf16[64,2,720]{2,1,0:T(2,128)(2,1)} %param.14) | copy-start | bytes 552964
  35.9 7.3 copy-start.21
  39.9 451.7 %all-reduce.2.cloned.1.call-start = ((), (), s32[]{:S(2)}) async-start(), calls=%async_computation.4 | async-start | bytes 1474560 | tf_op jit(solution)/shard_map/psum | solution.py:147
  50.1 8.7 copy-start.18
  314.4 6.5 copy-start.3
  331.0 6.5 copy-start.3
  347.7 6.5 copy-start.3
  364.3 6.5 copy-start.3
  397.6 6.5 copy-start.3
  430.9 6.5 copy-start.3
  443.2 49.9 %copy-start.19 = (f32[2880]{0:T(1024)S(1)}, f32[2880]{0:T(1024)}, u32[]{:S(2)}) copy-start(f32[2880]{0:T(1024)} %param.23) | copy-start | bytes 34564
  444.3 398.4 %reduce-scatter.2.cloned.1.call-start = ((), (), s32[]{:S(2)}) async-start(), calls=%async_computation.5 | async-start | bytes 9216000 | tf_op jit(solution)/shard_map/reduce_scatter | solution.py:187
  753.5 10.1 %copy-start.26 = (bf16[1,360,2880]{2,1,0:T(8,128)(2,1)S(1)}, bf16[1,360,2880]{2,1,0:T(8,128)(2,1)}, u32[]{:S(2)}) copy-start(bf16[1,360,2880]{2,1,0:T(8,128)(2,1)} %param.25) | copy-start | bytes 6220804
  850.6 11.8 %copy-start.23 = (f32[64,2,4]{0,2,1:T(4,128)S(1)}, f32[64,2,4]{0,2,1:T(4,128)}, u32[]{:S(2)}) copy-start(f32[64,2,4]{0,2,1:T(4,128)} %param.22) | copy-start | bytes 6148
  850.6 11.9 %copy-start.7 = (bf16[128,1,32]{2,0,1:T(8,128)(2,1)S(1)}, bf16[128,1,32]{2,0,1:T(8,128)(2,1)}, u32[]{:S(2)}) copy-start(bf16[128,1,32]{2,0,1:T(8,128)(2,1)} %copy-done.6) | copy-start | bytes 24580
  850.6 11.9 %copy-start.9 = (bf16[128,1,32]{2,0,1:T(8,128)(2,1)S(1)}, bf16[128,1,32]{2,0,1:T(8,128)(2,1)}, u32[]{:S(2)}) copy-start(bf16[128,1,32]{2,0,1:T(8,128)(2,1)} %copy-done.8) | copy-start | bytes 24580
  850.6 11.9 %copy-start.11 = (bf16[128,1,64]{2,0,1:T(8,128)(2,1)S(1)}, bf16[128,1,64]{2,0,1:T(8,128)(2,1)}, u32[]{:S(2)}) copy-start(bf16[128,1,64]{2,0,1:T(8,128)(2,1)} %copy-done.10) | copy-start | bytes 49156
  850.6 69.2 %all-to-all-start.1 = ((bf16[64,20,720]{2,1,0:T(8,128)(2,1)}), bf16[64,20,720]{2,1,0:T(8,128)(2,1)}, u32[]{:S(2)}, u32[]{:S(2)}) async-start(bf16[64,20,720]{2,1,0:T(8,128)(2,1)} %convert_element_type.115), calls=%async_computation.2 | async-start | bytes 4718592 | tf_op jit(solution)/shard_map/all_to_all | solution.py:190
  (42 other events, 203.3 us)
Sparse Core Ops, SparseCore 0:
  40.0 267.3 all-gather.1
  444.4 47.1 all-reduce.1
  770.6 72.0 reduce-scatter.1
where the time goes:
time: 947 us; the launch traced here: 944 us
  waiting for transfers between devices  419 us (44%)
  blocking collectives  227 us (24%)
  matrix products  116 us (12%)
  local copies, waits for them, and re-layouts  103 us (11%)
  other arithmetic  51.9 us (5%)
  between operations  14.1 us (1%)
  starting transfers between devices  12.3 us (1%)
    all_gather x1, waiting for transfers between devices, on_device(): key_piece = lax.all_gather(joined, 'expert', axis=0, tiled=True)  248 us
    all_to_all x1, blocking collectives, on_device(): lax.all_to_all(outgoing.reshape(expert_count, capacity, model_width), 'ex...  213 us
    reduce_scatter x1, waiting for transfers between devices, on_device(): lax.psum_scatter(partial_value.astype(jnp.bfloat16), 'tensor', scatter_di...  72.2 us
    all_to_all x1, waiting for transfers between devices, on_device(): lax.all_to_all(owner_sums.reshape(expert_count, capacity, quarter).astype...  54.2 us
    dot_general x8, matrix products, one_block(): jnp.einsum('shqd,kshd->shqk', query_heads, key_block[..., :head_dim], pre...  47.7 us
    dot_general x8, matrix products, one_block(): jnp.einsum('shqk,kshd->shqd', weights.astype(jnp.bfloat16), key_block[......  45.1 us
    psum x1, waiting for transfers between devices, on_device(): hidden_sum = lax.psum(residual_term.astype(jnp.bfloat16), 'tensor')  45 us
    reduce_sum x8, other arithmetic, one_block(): next_sum = running_sum * shrink_factor + jnp.sum(weights, axis=-1)  24.9 us
  transfers between devices with their start and end apart: 4, of which 4 were waited for; matrix products, arithmetic and copies ran while one was open for 3% of the time, Pallas kernels for 0%

commit v1 on v0

--- a/solution.py
+++ b/solution.py
@@ -1,12 +1,279 @@
+import functools
 import math
 
 import jax
 import jax.numpy as jnp
 from jax import lax
+from jax.experimental import pallas as pl
+from jax.experimental.pallas import tpu as pltpu
 from jax.sharding import PartitionSpec as P
 
 EPSILON = 1e-05
 ROPE_BASE = 150000.0
+NEG = -1e30
+MESH = pl.DeviceIdType.MESH
+NY, NX, NZ = 2, 4, 8
+LOG2E = 1.4426950408889634
+
+
+def place_of(expert_rank):
+    return expert_rank // (NX * NZ), (expert_rank // NZ) % NX, expert_rank % NZ
+
+
+def rank_of(y_lo, x, z):
+    return (y_lo * NX + x) * NZ + z
+
+
+def greet(devices):
+    barrier = pltpu.get_barrier_semaphore()
+    for device in devices:
+        pl.semaphore_signal(barrier, inc=1, device_id=device, device_id_type=MESH)
+    pl.semaphore_wait(barrier, len(devices))
+
+
+def send(src, dst, send_sem, recv_sem, device):
+    copy = pltpu.make_async_remote_copy(
+        src_ref=src,
+        dst_ref=dst,
+        send_sem=send_sem,
+        recv_sem=recv_sem,
+        device_id=device,
+        device_id_type=MESH,
+    )
+    copy.start()
+    return copy
+
+
+def arrived(dst, send_sem, recv_sem, device):
+    pltpu.make_async_remote_copy(
+        src_ref=dst,
+        dst_ref=dst,
+        send_sem=send_sem,
+        recv_sem=recv_sem,
+        device_id=device,
+        device_id_type=MESH,
+    ).wait_recv()
+
+
+def exchange_kernel(kv, q, kv_all, q_all, own_sem, xs, xr, ys, yr, zs, zr):
+    rank, tensor = lax.axis_index("expert"), lax.axis_index("tensor")
+    y_lo, x, z = place_of(rank)
+    other = 1 - y_lo
+    x_peers = [(rank_of(y_lo, lax.rem(x + d, NX), z), tensor) for d in range(1, NX)]
+    y_peer = (rank_of(other, x, z), tensor)
+    ring = [
+        (rank_of(y_lo, x, lax.rem(z + 1, NZ)), tensor),
+        (rank_of(y_lo, x, lax.rem(z + NZ - 1, NZ)), tensor),
+    ]
+    greet(x_peers + [y_peer] + ring)
+    own = [
+        pltpu.make_async_copy(kv, kv_all.at[z * 2 + y_lo], own_sem.at[0]),
+        pltpu.make_async_copy(q, q_all.at[x], own_sem.at[1]),
+    ]
+    for copy in own:
+        copy.start()
+    pending = [send(kv, kv_all.at[z * 2 + y_lo], ys.at[0], yr.at[0], y_peer)]
+
+    def slot(direction, steps, piece):
+        origin = lax.rem(z + (NZ - steps if direction == 0 else steps), NZ)
+        return kv_all.at[origin * 2 + (y_lo if piece == 0 else other)]
+
+    def sems(direction, step, piece):
+        index = 2 * (step - 1) + piece
+        return zs.at[direction, index], zr.at[direction, index]
+
+    def pass_on(direction, step, piece):
+        src = kv if step == 1 and piece == 0 else slot(direction, step - 1, piece)
+        pending.append(
+            send(src, slot(direction, step - 1, piece), *sems(direction, step, piece), ring[direction])
+        )
+
+    def got(direction, step, piece):
+        arrived(slot(direction, step, piece), *sems(direction, step, piece), ring[direction])
+
+    for direction in range(2):
+        pass_on(direction, 1, 0)
+    for d in range(1, NX):
+        pending.append(send(q, q_all.at[x], xs.at[d - 1], xr.at[d - 1], x_peers[d - 1]))
+    arrived(kv_all.at[z * 2 + other], ys.at[0], yr.at[0], y_peer)
+    for direction in range(2):
+        pass_on(direction, 1, 1)
+    half = NZ // 2
+    for step in range(2, half + 1):
+        for piece in range(2):
+            for direction in range(2):
+                got(direction, step - 1, piece)
+                if step < half or direction == piece:
+                    pass_on(direction, step, piece)
+    for direction in range(2):
+        got(direction, half, direction)
+    for d in range(1, NX):
+        arrived(q_all.at[lax.rem(x + NX - d, NX)], xs.at[d - 1], xr.at[d - 1], x_peers[d - 1])
+    for copy in own:
+        copy.wait()
+    for copy in pending:
+        copy.wait_send()
+
+
+def exchange(kv, q):
+    return pl.pallas_call(
+        exchange_kernel,
+        out_shape=(
+            jax.ShapeDtypeStruct((NY * NZ,) + kv.shape, kv.dtype),
+            jax.ShapeDtypeStruct((NX,) + q.shape, q.dtype),
+        ),
+        in_specs=[pl.BlockSpec(memory_space=pl.ANY)] * 2,
+        out_specs=(pl.BlockSpec(memory_space=pl.ANY),) * 2,
+        scratch_shapes=[
+            pltpu.SemaphoreType.DMA((2,)),
+            pltpu.SemaphoreType.DMA((NX - 1,)),
+            pltpu.SemaphoreType.DMA((NX - 1,)),
+            pltpu.SemaphoreType.DMA((1,)),
+            pltpu.SemaphoreType.DMA((1,)),
+            pltpu.SemaphoreType.DMA((2, NZ)),
+            pltpu.SemaphoreType.DMA((2, NZ)),
+        ],
+        compiler_params=pltpu.CompilerParams(collective_id=0, has_side_effects=True),
+        name="exchange",
+    )(kv, q)
+
+
+def attend_kernel(my_x, q_ref, kv_ref, mask_ref, o_ref, stat_ref, vt_ref, qa_ref):
+    xq = pl.program_id(1)
+    chunks, _, chunk = vt_ref.shape
+    shards, _, keys, width = kv_ref.shape
+    per = chunk // keys
+    head, cols = q_ref.shape[2:]
+
+    @pl.when(xq == 0)
+    def _():
+        for j in range(chunks):
+            rows = kv_ref[j * per : (j + 1) * per, 0].reshape(chunk, width)
+            flipped = rows.astype(jnp.float32).T
+            vt_ref[j, :16, :] = jnp.ones((16, chunk), jnp.bfloat16)
+            vt_ref[j, 16:, :] = flipped[head:].astype(jnp.bfloat16)
+
+    qa_ref[:head, :] = q_ref[0, 0]
+    qa_ref[head:width, :] = jnp.zeros((width - head, cols), jnp.bfloat16)
+    row = lax.broadcasted_iota(jnp.int32, (width, cols), 0)
+    lane = lax.broadcasted_iota(jnp.int32, (width, cols), 1)
+    span = head
+    tri = jnp.where(xq == my_x[0], lane % span, -1)
+    hot = (row == tri) | (row == span + xq) | (row == span + NX)
+    qa_ref[width:, :] = jnp.where(hot, 1.0, 0.0).astype(jnp.bfloat16)
+    qa = qa_ref[...]
+    top = jnp.full((1, cols), -3e38, jnp.float32)
+    acc = jnp.zeros((vt_ref.shape[1], cols), jnp.float32)
+    for j in range(chunks):
+        lhs = jnp.concatenate(
+            [
+                kv_ref[j * per : (j + 1) * per, 0].reshape(chunk, width),
+                mask_ref[0, j * per : (j + 1) * per].reshape(chunk, width),
+            ],
+            axis=1,
+        )
+        scores = jnp.dot(lhs, qa, preferred_element_type=jnp.float32)
+        new_top = jnp.maximum(top, jnp.max(scores, axis=0, keepdims=True))
+        probs = jnp.exp2(scores - new_top).astype(jnp.bfloat16)
+        acc = acc * jnp.exp2(top - new_top) + jnp.dot(
+            vt_ref[j], probs, preferred_element_type=jnp.float32
+        )
+        top = new_top
+    total = acc[0:1]
+    o_ref[0, 0] = (acc[16:] / total).astype(jnp.bfloat16)
+    stat_ref[0, 0, 0:1, :] = top
+    stat_ref[0, 0, 1:2, :] = total
+    stat_ref[0, 0, 2:, :] = jnp.zeros((6, cols), jnp.float32)
+
+
+def attend(my_x, q_all, kv_all, mask):
+    nx, seqs, head, cols = q_all.shape
+    shards, _, keys, width = kv_all.shape
+    chunk = 2 * keys
+    chunks = shards * keys // chunk
+    return pl.pallas_call(
+        attend_kernel,
+        grid=(seqs, nx),
+        in_specs=[
+            pl.BlockSpec(memory_space=pltpu.SMEM),
+            pl.BlockSpec((1, 1, head, cols), lambda s, i: (i, s, 0, 0)),
+            pl.BlockSpec((shards, 1, keys, width), lambda s, i: (0, s, 0, 0)),
+            pl.BlockSpec((1, shards, keys, width), lambda s, i: (s, 0, 0, 0)),
+        ],
+        out_shape=(
+            jax.ShapeDtypeStruct((nx, seqs, head, cols), jnp.bfloat16),
+            jax.ShapeDtypeStruct((nx, seqs, 8, cols), jnp.float32),
+        ),
+        out_specs=(
+            pl.BlockSpec((1, 1, head, cols), lambda s, i: (i, s, 0, 0)),
+            pl.BlockSpec((1, 1, 8, cols), lambda s, i: (i, s, 0, 0)),
+        ),
+        scratch_shapes=[
+            pltpu.VMEM((chunks, 16 + head, chunk), jnp.bfloat16),
+            pltpu.VMEM((2 * width, cols), jnp.bfloat16),
+        ],
+        compiler_params=pltpu.CompilerParams(vmem_limit_bytes=48 * 1024 * 1024),
+        name="attend",
+    )(my_x, q_all, kv_all, mask)
+
+
+def back_kernel(o, stat, o_in, stat_in, own_sem, os, orr, ss, sr):
+    rank, tensor = lax.axis_index("expert"), lax.axis_index("tensor")
+    y_lo, x, z = place_of(rank)
+    peers = [(rank_of(y_lo, lax.rem(x + d, NX), z), tensor) for d in range(1, NX)]
+    greet(peers)
+    own = [
+        pltpu.make_async_copy(o.at[x], o_in.at[x], own_sem.at[0]),
+        pltpu.make_async_copy(stat.at[x], stat_in.at[x], own_sem.at[1]),
+    ]
+    for copy in own:
+        copy.start()
+    pending = []
+    for d in range(1, NX):
+        to = lax.rem(x + d, NX)
+        pending.append(send(o.at[to], o_in.at[x], os.at[d - 1], orr.at[d - 1], peers[d - 1]))
+        pending.append(send(stat.at[to], stat_in.at[x], ss.at[d - 1], sr.at[d - 1], peers[d - 1]))
+    for d in range(1, NX):
+        source = lax.rem(x + NX - d, NX)
+        arrived(o_in.at[source], os.at[d - 1], orr.at[d - 1], peers[d - 1])
+        arrived(stat_in.at[source], ss.at[d - 1], sr.at[d - 1], peers[d - 1])
+    for copy in own:
+        copy.wait()
+    for copy in pending:
+        copy.wait_send()
+
+
+def send_back(o, stat):
+    return pl.pallas_call(
+        back_kernel,
+        out_shape=(
+            jax.ShapeDtypeStruct(o.shape, o.dtype),
+            jax.ShapeDtypeStruct(stat.shape, stat.dtype),
+        ),
+        in_specs=[pl.BlockSpec(memory_space=pl.ANY)] * 2,
+        out_specs=(pl.BlockSpec(memory_space=pl.ANY),) * 2,
+        scratch_shapes=[pltpu.SemaphoreType.DMA((2,))]
+        + [pltpu.SemaphoreType.DMA((NX - 1,))] * 4,
+        compiler_params=pltpu.CompilerParams(collective_id=1, has_side_effects=True),
+        name="send_back",
+    )(o, stat)
+
+
+def key_masks(prefix_length, expert_rank, cache_rows, span, width):
+    y_lo, x, z = place_of(expert_rank)
+    shape = (prefix_length.shape[0], NY * NZ, cache_rows + span, width)
+    shard = lax.broadcasted_iota(jnp.int32, shape, 1)
+    row = lax.broadcasted_iota(jnp.int32, shape, 2)
+    col = lax.broadcasted_iota(jnp.int32, shape, 3)
+    key_rank = rank_of(shard % 2, x, shard // 2)
+    in_cache = row < cache_rows
+    beyond = (key_rank * cache_rows + row >= prefix_length[:, None, None, None]) & (
+        col == span + NX
+    )
+    later_block = (col >= span) & (col < span + NX) & (key_rank > rank_of(y_lo, col - span, z))
+    later_key = (col < span) & (key_rank == expert_rank) & (row - cache_rows > col)
+    blocked = jnp.where(in_cache, beyond, later_block | later_key)
+    return jnp.where(blocked, NEG, 0.0).astype(jnp.bfloat16)
 
 
 def rotate(vectors, places):
@@ -62,11 +329,15 @@
     inverse_square_root = lax.rsqrt(square_sum / model_width + EPSILON)
     span_place = expert_rank * span_dev + jnp.arange(span_dev, dtype=jnp.int32)
     places = (prefix_length[None, :] + span_place[:, None]).reshape(row_count).astype(jnp.float32)
-    query_matrix = rotate(
-        (query_acc * inverse_square_root[:, None]).reshape(
-            row_count, query_cols // head_dim, head_dim
-        ),
-        places[:, None],
+    query_scale = head_dim ** (-0.5) * LOG2E
+    query_matrix = (
+        rotate(
+            (query_acc * inverse_square_root[:, None]).reshape(
+                row_count, query_cols // head_dim, head_dim
+            ),
+            places[:, None],
+        )
+        * query_scale
     ).astype(jnp.bfloat16)
     key_value_heads = (keyval_acc * inverse_square_root[:, None]).reshape(
         row_count, local_kv, 2 * head_dim
@@ -77,66 +348,24 @@
     ).astype(jnp.bfloat16)
     new_key_value_rows = new_key_value_rows.reshape(span_dev, seq_count, local_kv, 2 * head_dim)
     query_count = span_dev * group_width
-    query_heads = query_matrix.reshape(
-        span_dev, seq_count, local_kv, group_width, head_dim
-    ).transpose(1, 2, 0, 3, 4)
-    query_heads = query_heads.reshape(seq_count, local_kv, query_count, head_dim)
-    query_place = expert_rank * span_dev + jnp.arange(query_count, dtype=jnp.int32) // group_width
-    stride = cache_rows + span_dev
-    score_scale = head_dim ** (-0.5)
-    joined = jnp.concatenate([cache_keyval, new_key_value_rows], axis=0)
-    start_state = (
-        jnp.full((seq_count, local_kv, query_count), -1e30, jnp.float32),
-        jnp.zeros((seq_count, local_kv, query_count), jnp.float32),
-        jnp.zeros((seq_count, local_kv, query_count, head_dim), jnp.float32),
-    )
-    key_piece = lax.all_gather(joined, "expert", axis=0, tiled=True)
-    key_count = key_piece.shape[0]
-    block_size = math.gcd(key_count, 2048)
-
-    def one_block(loop_index, running):
-        running_max, running_sum, running_out = running
-        key_block = lax.dynamic_slice_in_dim(key_piece, loop_index * block_size, block_size, 0)
-        global_row = loop_index * block_size + jnp.arange(block_size, dtype=jnp.int32)
-        source_dev = global_row // stride
-        offset = global_row % stride
-        in_cache = offset < cache_rows
-        cache_place = source_dev * cache_rows + offset
-        key_place = source_dev * span_dev + offset - cache_rows
-        scores = (
-            jnp.einsum(
-                "shqd,kshd->shqk",
-                query_heads,
-                key_block[..., :head_dim],
-                preferred_element_type=jnp.float32,
-            )
-            * score_scale
-        )
-        cache_ok = cache_place[None, :] < prefix_length[:, None]
-        span_ok = key_place[None, :] <= query_place[:, None]
-        allowed = jnp.where(
-            in_cache[None, None, None, :], cache_ok[:, None, None, :], span_ok[None, None, :, :]
-        )
-        masked = jnp.where(allowed, scores, -1e30)
-        next_max = jnp.maximum(running_max, jnp.max(masked, axis=-1))
-        weights = jnp.where(allowed, jnp.exp(masked - next_max[..., None]), 0.0)
-        shrink_factor = jnp.exp(running_max - next_max)
-        next_sum = running_sum * shrink_factor + jnp.sum(weights, axis=-1)
-        next_out = running_out * shrink_factor[..., None] + jnp.einsum(
-            "shqk,kshd->shqd",
-            weights.astype(jnp.bfloat16),
-            key_block[..., head_dim:],
-            preferred_element_type=jnp.float32,
-        )
-        return (next_max, next_sum, next_out)
-
-    final_max, final_sum, final_out = lax.fori_loop(
-        0, key_count // block_size, one_block, start_state
-    )
-    attended = (final_out / final_sum[..., None]).astype(jnp.bfloat16)
+    own_queries = query_matrix.reshape(span_dev, seq_count, group_width, head_dim).transpose(
+        1, 3, 2, 0
+    )
+    own_queries = own_queries.reshape(seq_count, head_dim, query_count)
+    joined = jnp.concatenate([cache_keyval, new_key_value_rows], axis=0)[:, :, 0, :]
+    joined = joined.transpose(1, 0, 2)
+    kv_all, q_all = exchange(joined, own_queries)
+    mask = key_masks(prefix_length, expert_rank, cache_rows, span_dev, 2 * head_dim)
+    my_x = place_of(expert_rank)[1].astype(jnp.int32).reshape(1)
+    part, stat = attend(my_x, q_all, kv_all, mask)
+    part, stat = send_back(part, stat)
+    tops, sums = stat[:, :, 0, :], stat[:, :, 1, :]
+    share = jnp.exp2(tops - jnp.max(tops, axis=0)) * sums
+    share = share / jnp.sum(share, axis=0)
+    attended = jnp.sum(part.astype(jnp.float32) * share[:, :, None, :], axis=0).astype(jnp.bfloat16)
     attended = (
-        attended.reshape(seq_count, local_kv, span_dev, group_width, head_dim)
-        .transpose(2, 0, 1, 3, 4)
+        attended.reshape(seq_count, head_dim, group_width, span_dev)
+        .transpose(3, 0, 2, 1)
         .reshape(row_count, query_cols)
     )
     projected = jnp.dot(attended, w_out, preferred_element_type=jnp.float32)

time: 947 us -> 659 us (0.70)
  waiting for transfers between devices: 419 us -> 170 us
  matrix products: 116 us -> 23.5 us
  Pallas kernels: 0 us -> 75.7 us
  other arithmetic: 51.9 us -> 30.3 us
    all_gather x1 -> x0, waiting for transfers between devices: 248 us -> none  [on_device(): key_piece = lax.all_gather(joined, 'expert', axis=0, tiled=True)]
    dot_general x16 -> x0, matrix products: 92.8 us -> none  [the longest x8 47.7 us: one_block(): jnp.einsum('shqd,kshd->shqk', query_heads, key_block[..., :head_dim], pre...]
    pallas_call x0 -> x3, Pallas kernels: none -> 75.7 us  [the longest x1 33.6 us: attend(): pl.pallas_call(attend_kernel, grid=(seqs, nx), in_specs=[pl.BlockSpec(mem...]
    reduce_sum x8 -> x2, other arithmetic: 24.9 us -> 1.9 us  [the longest x1 1.15 us: on_device(): jnp.sum(part.astype(jnp.float32) * share[:, :, None, :], axis=0)]
  transfers between devices with their start and end apart: 4 -> 3, of which waited for: 4 -> 3; matrix products, arithmetic and copies ran while one was open for 3% -> 1% of each run, Pallas kernels for 0% -> 0%
where the time goes in v1:
time: 659 us; the launch traced here: 650 us
  blocking collectives  227 us (34%)
  waiting for transfers between devices  170 us (26%)
  local copies, waits for them, and re-layouts  96.6 us (15%)
  Pallas kernels  75.7 us (11%)
  other arithmetic  30.3 us (5%)
  matrix products  23.5 us (4%)
  between operations  14.8 us (2%)
  starting transfers between devices  11.7 us (2%)
    all_to_all x1, blocking collectives, on_device(): lax.all_to_all(outgoing.reshape(expert_count, capacity, model_width), 'ex...  213 us
    reduce_scatter x1, waiting for transfers between devices, on_device(): lax.psum_scatter(partial_value.astype(jnp.bfloat16), 'tensor', scatter_di...  72.2 us
    all_to_all x1, waiting for transfers between devices, on_device(): lax.all_to_all(owner_sums.reshape(expert_count, capacity, quarter).astype...  54.2 us
    psum x1, waiting for transfers between devices, on_device(): hidden_sum = lax.psum(residual_term.astype(jnp.bfloat16), 'tensor')  44 us
    pallas_call x1, Pallas kernels, attend(): pl.pallas_call(attend_kernel, grid=(seqs, nx), in_specs=[pl.BlockSpec(mem...  33.6 us
    pallas_call x1, Pallas kernels, exchange(): pl.pallas_call(exchange_kernel, out_shape=(jax.ShapeDtypeStruct((NY * NZ,...  33 us
    all_gather x1, blocking collectives, on_device(): shard_piece = lax.all_gather(tokens, 'tensor', axis=2, tiled=True)  13.9 us
  transfers between devices with their start and end apart: 3, of which 3 were waited for; matrix products, arithmetic and copies ran while one was open for 1% of the time, Pallas kernels for 0%

profile of v1, /device:TPU:40, one launch (start us, length us, event | category | flops | bytes accessed | tf_op | source)
XLA Modules:
  0.0 649.8 jit_solution(14297325101747823420)
XLA Ops:
  12.9 13.9 %all_gather.3 = bf16[64,2,2880]{0,1,2:T(2,128)(2,1)} all-gather(bf16[64,2,720]{0,1,2:T(2,128)(2,1)S(1)} %copy.126), channel_id=1, replica_groups=mesh['expert'=64,'tensor'=4] {'tensor'}, dimensions={2}, use_global_device_ids=true | all-gather | bytes 921600 | tf_op jit(solution)/shard_map/all_gather | solution.py:321
  26.9 4.2 copy.127
  31.1 3.0 copy.138
  36.6 2.8 copy.128
  39.4 2.9 convert_element_type.94
  44.4 3.2 reshape.337
  47.6 2.9 convolution_multiply_fusion
  60.5 33.0 %exchange.1 = (bf16[16,2,256,128]{3,2,1,0:T(8,128)(2,1)}, bf16[4,2,64,512]{3,2,1,0:T(8,128)(2,1)}) custom-call(bf16[2,256,128]{2,1,0:T(8,128)(2,1)} %maximum_bitcast_fusion.kv, bf16[2,64,512]{2,1,0:T(8,128)(2,1)} %reshape.327.q), custom_call_target="tpu_custom_call" | custom-call | tf_op jit(solution)/shard_map/exchange/pallas_call | solution.py:119
  97.2 33.6 %attend.1 = (bf16[4,2,64,512]{3,2,1,0:T(8,128)(2,1)S(1)}, f32[4,2,8,512]{3,2,1,0:T(8,128)S(1)}) custom-call(s32[1]{0:T(128)} %bitcast.my_x, bf16[4,2,64,512]{3,2,1,0:T(8,128)(2,1)S(1)} %copy-done.3, bf16[16,2,256,128]{3,2,1,0:T(8,128)(2,1)S(1)} %copy-done.2, bf16[2,16,256,128]{3,2,1,0:T(8,128)(2,1)S(1)} %select_convert_fusion.mask_ref), custom_call_target="tpu_custom_call" | custom-call | tf_op jit(solution)/shard_map/attend/pallas_call | solution.py:194
  132.3 9.0 %send_back.1 = (bf16[4,2,64,512]{3,2,1,0:T(8,128)(2,1)}, f32[4,2,8,512]{3,2,1,0:T(8,128)}) custom-call(bf16[4,2,64,512]{3,2,1,0:T(8,128)(2,1)} %copy-done.4, f32[4,2,8,512]{3,2,1,0:T(8,128)} %copy-done.5), custom_call_target="tpu_custom_call" | custom-call | tf_op jit(solution)/shard_map/send_back/pallas_call | solution.py:247
  161.0 44.0 %all-reduce.2.cloned.1.call-done = bf16[128,2880]{0,1:T(8,128)(2,1)} async-done(((bf16[128,2880]{0,1:T(8,128)(2,1)}), bf16[128,2880]{0,1:T(8,128)(2,1)}) %all-reduce.2.cloned.1.call-update) | async-done | bytes 737296 | tf_op jit(solution)/shard_map/psum | solution.py:376
  210.9 5.6 reshape.353
  216.5 10.3 %scatter_custom_fusion = bf16[1280,2880]{1,0:T(8,128)(2,1)} fusion(s32[512]{0:T(512)S(1)} %bitcast.78, bf16[512,2880]{1,0:T(8,128)(2,1)} %reshape.353, bf16[]{:T(256)} %constant.131.clone.1), kind=kCustom, calls=%fused_computation.15 | custom fusion | bytes 7373312 | tf_op jit(solution)/shard_map/scatter | solution.py:395
  226.9 11.9 %reshape.331 = bf16[64,20,2880]{2,1,0:T(8,128)(2,1)} reshape(bf16[1280,2880]{1,0:T(8,128)(2,1)} %scatter_custom_fusion) | data formatting | bytes 14745600 | tf_op jit(solution)/shard_map/reshape | solution.py:398
  238.7 212.9 %all_to_all.10 = bf16[64,20,2880]{2,1,0:T(8,128)(2,1)} all-to-all(bf16[64,20,2880]{2,1,0:T(8,128)(2,1)} %reshape.331), channel_id=1, replica_groups=mesh['expert'=64,'tensor'=4] {'expert'}, dimensions={0} | all-to-all | bytes 14745600 | tf_op jit(solution)/shard_map/all_to_all | solution.py:397
  451.6 12.0 %reshape.332 = bf16[1280,2880]{1,0:T(8,128)(2,1)} reshape(bf16[64,20,2880]{2,1,0:T(8,128)(2,1)} %all_to_all.10) | data formatting | bytes 14745600 | tf_op jit(solution)/shard_map/reshape | solution.py:405
  463.6 10.1 %fusion.41 = f32[1280,720]{0,1:T(8,128)S(1)} fusion(bf16[1280,2880]{1,0:T(8,128)(2,1)} %reshape.332, bf16[2880,720]{0,1:T(8,128)(2,1)} %bitcast.80), kind=kOutput, calls=%fused_computation.99 | convolution fusion | flops 5308416000 | bytes 15206400 | tf_op jit(solution)/shard_map/dot_general | solution.py:404
  473.7 6.8 %convolution_convert_fusion = bf16[1280,2880]{0,1:T(8,128)(2,1)} fusion(bf16[1,360,2880]{2,1,0:T(8,128)(2,1)S(1)} %copy-done.19, f32[1280,720]{0,1:T(8,128)S(1)} %fusion.41), kind=kOutput, calls=%fused_computation.2 | convolution fusion | flops 2661580800 | bytes 13132800 | tf_op jit(solution)/shard_map/dot_general | solution.py:414
  480.5 72.2 %reduce-scatter.2.cloned.1.call-done = bf16[1280,720]{0,1:T(8,128)(2,1)} async-done(((bf16[1280,2880]{0,1:T(8,128)(2,1)}), bf16[1280,720]{0,1:T(8,128)(2,1)}) %reduce-scatter.2.cloned.1.call-update) | async-done | bytes 1843216 | tf_op jit(solution)/shard_map/reduce_scatter | solution.py:416
  552.7 2.6 copy.152
  557.4 11.6 %all-to-all-start.1 = ((bf16[64,20,720]{2,1,0:T(8,128)(2,1)}), bf16[64,20,720]{2,1,0:T(8,128)(2,1)S(1)}, u32[]{:S(2)}, u32[]{:S(2)}) async-start(bf16[64,20,720]{2,1,0:T(8,128)(2,1)} %convert_element_type.114), calls=%async_computation.2 | async-start | bytes 4718592 | tf_op jit(solution)/shard_map/all_to_all | solution.py:419
  572.3 54.2 %all-to-all-done.1 = bf16[64,20,720]{2,1,0:T(8,128)(2,1)S(1)} async-done(((bf16[64,20,720]{2,1,0:T(8,128)(2,1)}), bf16[64,20,720]{2,1,0:T(8,128)(2,1)S(1)}, u32[]{:S(2)}, u32[]{:S(2)}) %all-to-all-start.1) | async-done | bytes 1843232 | tf_op jit(solution)/shard_map/all_to_all | solution.py:419
  629.2 5.3 gather_fusion
  634.5 2.9 reshape.335
  (125 shorter events, 64.1 us)
Async XLA Ops:
  7.2 145.1 %copy-start = (bf16[512,2880]{0,1:T(8,128)(2,1)S(1)}, bf16[512,2880]{0,1:T(8,128)(2,1)}, u32[]{:S(2)}) copy-start(bf16[512,2880]{0,1:T(8,128)(2,1)} %param.16) | copy-start | bytes 8847364
  7.2 197.8 %all-reduce.2.cloned.1.call-start = ((), (), s32[]{:S(2)}) async-start(), calls=%async_computation.3 | async-start | bytes 1474560 | tf_op jit(solution)/shard_map/psum | solution.py:376
  12.9 21.2 %copy-start.14 = (f32[2880]{0:T(1024)S(1)}, f32[2880]{0:T(1024)}, u32[]{:S(2)}) copy-start(f32[2880]{0:T(1024)} %param.13) | copy-start | bytes 34564
  50.4 43.2 %copy-start.18 = (s32[2]{0:T(128)S(1)}, s32[2]{0:T(128)}, u32[]{:S(2)}) copy-start(s32[2]{0:T(128)} %param.18) | copy-start | bytes 28
  58.5 72.3 %copy-start.8 = (bf16[64,2,1,32]{3,0,1,2:T(8,128)(2,1)}, bf16[64,2,1,32]{3,0,1,2:T(8,128)(2,1)S(1)}, u32[]{:S(2)}) copy-start(bf16[64,2,1,32]{3,0,1,2:T(8,128)(2,1)S(1)} %copy.134) | copy-start | bytes 24580
  58.7 72.1 %copy-start.10 = (bf16[64,2,1,32]{3,0,1,2:T(8,128)(2,1)}, bf16[64,2,1,32]{3,0,1,2:T(8,128)(2,1)S(1)}, u32[]{:S(2)}) copy-start(bf16[64,2,1,32]{3,0,1,2:T(8,128)(2,1)S(1)} %copy.135) | copy-start | bytes 24580
  58.8 72.0 %copy-start.12 = (bf16[64,2,1,64]{3,0,1,2:T(8,128)(2,1)}, bf16[64,2,1,64]{3,0,1,2:T(8,128)(2,1)S(1)}, u32[]{:S(2)}) copy-start(bf16[64,2,1,64]{3,0,1,2:T(8,128)(2,1)S(1)} %copy.136) | copy-start | bytes 49156
  93.6 2.5 copy-start.2
  96.1 1.0 copy-start.3
  97.2 46.7 %copy-start.7 = (bf16[64,2,720]{2,1,0:T(2,128)(2,1)S(1)}, bf16[64,2,720]{2,1,0:T(2,128)(2,1)}, u32[]{:S(2)}) copy-start(bf16[64,2,720]{2,1,0:T(2,128)(2,1)} %param.12) | copy-start | bytes 552964
  130.8 0.8 copy-start.4
  131.6 0.7 copy-start.5
  152.3 2.1 copy-start.6
  154.4 4.2 copy-start.15
  154.4 52.2 %copy-start.16 = (f32[2880]{0:T(1024)S(1)}, f32[2880]{0:T(1024)}, u32[]{:S(2)}) copy-start(f32[2880]{0:T(1024)} %param.21) | copy-start | bytes 34564
  158.5 394.2 %reduce-scatter.2.cloned.1.call-start = ((), (), s32[]{:S(2)}) async-start(), calls=%async_computation.4 | async-start | bytes 9216000 | tf_op jit(solution)/shard_map/reduce_scatter | solution.py:416
  463.6 10.1 %copy-start.19 = (bf16[1,360,2880]{2,1,0:T(8,128)(2,1)S(1)}, bf16[1,360,2880]{2,1,0:T(8,128)(2,1)}, u32[]{:S(2)}) copy-start(bf16[1,360,2880]{2,1,0:T(8,128)(2,1)} %param.23) | copy-start | bytes 6220804
  557.4 11.6 %copy-start.17 = (f32[64,2,4]{0,2,1:T(4,128)S(1)}, f32[64,2,4]{0,2,1:T(4,128)}, u32[]{:S(2)}) copy-start(f32[64,2,4]{0,2,1:T(4,128)} %param.20) | copy-start | bytes 6148
  557.4 11.8 %copy-start.9 = (bf16[64,2,1,32]{3,0,1,2:T(8,128)(2,1)S(1)}, bf16[64,2,1,32]{3,0,1,2:T(8,128)(2,1)}, u32[]{:S(2)}) copy-start(bf16[64,2,1,32]{3,0,1,2:T(8,128)(2,1)} %copy-done.8) | copy-start | bytes 24580
  557.4 11.8 %copy-start.11 = (bf16[64,2,1,32]{3,0,1,2:T(8,128)(2,1)S(1)}, bf16[64,2,1,32]{3,0,1,2:T(8,128)(2,1)}, u32[]{:S(2)}) copy-start(bf16[64,2,1,32]{3,0,1,2:T(8,128)(2,1)} %copy-done.10) | copy-start | bytes 24580
  557.4 11.8 %copy-start.13 = (bf16[64,2,1,64]{3,0,1,2:T(8,128)(2,1)S(1)}, bf16[64,2,1,64]{3,0,1,2:T(8,128)(2,1)}, u32[]{:S(2)}) copy-start(bf16[64,2,1,64]{3,0,1,2:T(8,128)(2,1)} %copy-done.12) | copy-start | bytes 49156
  557.4 69.2 %all-to-all-start.1 = ((bf16[64,20,720]{2,1,0:T(8,128)(2,1)}), bf16[64,20,720]{2,1,0:T(8,128)(2,1)S(1)}, u32[]{:S(2)}, u32[]{:S(2)}) async-start(bf16[64,20,720]{2,1,0:T(8,128)(2,1)} %convert_element_type.114), calls=%async_computation.2 | async-start | bytes 4718592 | tf_op jit(solution)/shard_map/all_to_all | solution.py:419
  634.5 8.3 %copy-start.1 = (bf16[512,2880]{0,1:T(8,128)(2,1)S(1)}, bf16[512,2880]{0,1:T(8,128)(2,1)}, u32[]{:S(2)}) copy-start(bf16[512,2880]{0,1:T(8,128)(2,1)} %param.16) | copy-start | bytes 8847364
Sparse Core Ops, SparseCore 0:
  158.6 46.3 all-reduce.1
  480.6 71.9 reduce-scatter.1

commit v2 on v1

--- a/solution.py
+++ b/solution.py
@@ -55,20 +55,21 @@
     ).wait_recv()
 
 
-def exchange_kernel(kv, q, kv_all, q_all, own_sem, xs, xr, ys, yr, zs, zr):
+def exchange_kernel(
+    kv, q, slab, kv_all, q_all, slab_all, own_sem, xs, xr, ys, yr, zs, zr, ts, tr
+):
     rank, tensor = lax.axis_index("expert"), lax.axis_index("tensor")
     y_lo, x, z = place_of(rank)
     other = 1 - y_lo
     x_peers = [(rank_of(y_lo, lax.rem(x + d, NX), z), tensor) for d in range(1, NX)]
     y_peer = (rank_of(other, x, z), tensor)
-    ring = [
-        (rank_of(y_lo, x, lax.rem(z + 1, NZ)), tensor),
-        (rank_of(y_lo, x, lax.rem(z + NZ - 1, NZ)), tensor),
-    ]
-    greet(x_peers + [y_peer] + ring)
+    z_peers = [(rank_of(y_lo, x, lax.rem(z + d, NZ)), tensor) for d in range(1, NZ)]
+    ring = [z_peers[0], z_peers[-1]]
+    greet(x_peers + [y_peer] + z_peers)
     own = [
         pltpu.make_async_copy(kv, kv_all.at[z * 2 + y_lo], own_sem.at[0]),
         pltpu.make_async_copy(q, q_all.at[x], own_sem.at[1]),
+        pltpu.make_async_copy(slab.at[z], slab_all.at[z], own_sem.at[2]),
     ]
     for copy in own:
         copy.start()
@@ -95,6 +96,11 @@
         pass_on(direction, 1, 0)
     for d in range(1, NX):
         pending.append(send(q, q_all.at[x], xs.at[d - 1], xr.at[d - 1], x_peers[d - 1]))
+    for d in range(1, NZ):
+        to = lax.rem(z + d, NZ)
+        pending.append(
+            send(slab.at[to], slab_all.at[z], ts.at[d - 1], tr.at[d - 1], z_peers[d - 1])
+        )
     arrived(kv_all.at[z * 2 + other], ys.at[0], yr.at[0], y_peer)
     for direction in range(2):
         pass_on(direction, 1, 1)
@@ -109,33 +115,40 @@
         got(direction, half, direction)
     for d in range(1, NX):
         arrived(q_all.at[lax.rem(x + NX - d, NX)], xs.at[d - 1], xr.at[d - 1], x_peers[d - 1])
+    for d in range(1, NZ):
+        arrived(
+            slab_all.at[lax.rem(z + NZ - d, NZ)], ts.at[d - 1], tr.at[d - 1], z_peers[d - 1]
+        )
     for copy in own:
         copy.wait()
     for copy in pending:
         copy.wait_send()
 
 
-def exchange(kv, q):
+def exchange(kv, q, slab):
     return pl.pallas_call(
         exchange_kernel,
         out_shape=(
             jax.ShapeDtypeStruct((NY * NZ,) + kv.shape, kv.dtype),
             jax.ShapeDtypeStruct((NX,) + q.shape, q.dtype),
+            jax.ShapeDtypeStruct(slab.shape, slab.dtype),
         ),
-        in_specs=[pl.BlockSpec(memory_space=pl.ANY)] * 2,
-        out_specs=(pl.BlockSpec(memory_space=pl.ANY),) * 2,
+        in_specs=[pl.BlockSpec(memory_space=pl.ANY)] * 3,
+        out_specs=(pl.BlockSpec(memory_space=pl.ANY),) * 3,
         scratch_shapes=[
-            pltpu.SemaphoreType.DMA((2,)),
+            pltpu.SemaphoreType.DMA((3,)),
             pltpu.SemaphoreType.DMA((NX - 1,)),
             pltpu.SemaphoreType.DMA((NX - 1,)),
             pltpu.SemaphoreType.DMA((1,)),
             pltpu.SemaphoreType.DMA((1,)),
             pltpu.SemaphoreType.DMA((2, NZ)),
             pltpu.SemaphoreType.DMA((2, NZ)),
+            pltpu.SemaphoreType.DMA((NZ - 1,)),
+            pltpu.SemaphoreType.DMA((NZ - 1,)),
         ],
         compiler_params=pltpu.CompilerParams(collective_id=0, has_side_effects=True),
         name="exchange",
-    )(kv, q)
+    )(kv, q, slab)
 
 
 def attend_kernel(my_x, q_ref, kv_ref, mask_ref, o_ref, stat_ref, vt_ref, qa_ref):
@@ -257,6 +270,480 @@
         compiler_params=pltpu.CompilerParams(collective_id=1, has_side_effects=True),
         name="send_back",
     )(o, stat)
+
+
+def corner(rank, tensor):
+    y_lo, x, z = place_of(rank)
+    y_hi, core = tensor // 2, lax.rem(tensor, 2)
+    far = (rank, (1 - y_hi) * 2 + core)
+    sides = [(rank_of(1 - y_lo, x, z), lax.rem(y_hi + r, 2) * 2 + core) for r in range(2)]
+    mate = (rank, y_hi * 2 + 1 - core)
+    return y_lo, x, z, y_hi, core, far, sides, mate
+
+
+def f32(value):
+    return value.astype(jnp.float32)
+
+
+def norm_kernel(
+    model_width, part, own_tokens, gain, hidden, spread,
+    core_in, core_out, far_in, squares, squares_in, own_sem, cs, cr, fs, fr, qs, qr, zs, zr,
+):
+    rank, tensor = lax.axis_index("expert"), lax.axis_index("tensor")
+    y_lo, x, z, y_hi, core, far, sides, mate = corner(rank, tensor)
+    cross = (rank, (1 - y_hi) * 2 + 1 - core)
+    ring = [
+        (rank_of(y_lo, x, lax.rem(z + 1, NZ)), tensor),
+        (rank_of(y_lo, x, lax.rem(z + NZ - 1, NZ)), tensor),
+    ]
+    greet([mate, far, cross] + ring)
+    pending = []
+    order = [1 - y_hi, y_hi]
+    for i in range(2):
+        src = part.at[order[i] * 2 + 1 - core]
+        pending.append(send(src, core_in.at[i], cs.at[i], cr.at[i], mate))
+    arrived(core_in.at[0], cs.at[0], cr.at[0], mate)
+    core_out[...] = (f32(part[order[0] * 2 + core]) + f32(core_in[0])).astype(jnp.bfloat16)
+    pending.append(send(core_out, far_in, fs.at[0], fr.at[0], far))
+    arrived(core_in.at[1], cs.at[1], cr.at[1], mate)
+    near = f32(own_tokens[...]) + (f32(part[order[1] * 2 + core]) + f32(core_in[1]))
+    arrived(far_in, fs.at[0], fr.at[0], far)
+    rounded = (near + f32(far_in[...])).astype(jnp.bfloat16)
+    hidden[...] = rounded
+    wide = f32(rounded)
+    own_squares = jnp.sum(wide * wide, axis=1, keepdims=True)
+    squares[...] = jnp.broadcast_to(own_squares, squares.shape)
+    trio = [mate, far, cross]
+    for i in range(3):
+        pending.append(send(squares, squares_in.at[i], qs.at[i], qr.at[i], trio[i]))
+    total = own_squares
+    for i in range(3):
+        arrived(squares_in.at[i], qs.at[i], qr.at[i], trio[i])
+        total = total + squares_in[i, :, 0:1]
+    root = lax.rsqrt(total / model_width + EPSILON)
+    spread[z] = (wide * root * gain[...]).astype(jnp.bfloat16)
+    rows = wide.shape[0] // 2
+
+    def slot(direction, steps, piece):
+        origin = lax.rem(z + (NZ - steps if direction == 0 else steps), NZ)
+        return spread.at[origin, pl.ds(piece * rows, rows)]
+
+    def sems(direction, step, piece):
+        index = 2 * (step - 1) + piece
+        return zs.at[direction, index], zr.at[direction, index]
+
+    def pass_on(direction, step, piece):
+        block = slot(direction, step - 1, piece)
+        pending.append(send(block, block, *sems(direction, step, piece), ring[direction]))
+
+    def got(direction, step, piece):
+        arrived(slot(direction, step, piece), *sems(direction, step, piece), ring[direction])
+
+    half = NZ // 2
+    for piece in range(2):
+        for direction in range(2):
+            pass_on(direction, 1, piece)
+    for step in range(2, half + 1):
+        for piece in range(2):
+            for direction in range(2):
+                got(direction, step - 1, piece)
+                if step < half or direction == piece:
+                    pass_on(direction, step, piece)
+    for direction in range(2):
+        got(direction, half, direction)
+    for copy in pending:
+        copy.wait_send()
+
+
+def norm_and_spread(part, own_tokens, gain, model_width):
+    rows, quarter = own_tokens.shape
+    block = (rows, quarter)
+    vmem = pl.BlockSpec(memory_space=pltpu.VMEM)
+    return pl.pallas_call(
+        functools.partial(norm_kernel, model_width),
+        out_shape=(
+            jax.ShapeDtypeStruct(block, jnp.bfloat16),
+            jax.ShapeDtypeStruct((NZ,) + block, jnp.bfloat16),
+        ),
+        in_specs=[vmem] * 3,
+        out_specs=(vmem, vmem),
+        scratch_shapes=[
+            pltpu.VMEM((2,) + block, jnp.bfloat16),
+            pltpu.VMEM(block, jnp.bfloat16),
+            pltpu.VMEM(block, jnp.bfloat16),
+            pltpu.VMEM((rows, 128), jnp.float32),
+            pltpu.VMEM((3, rows, 128), jnp.float32),
+            pltpu.SemaphoreType.DMA((1,)),
+            pltpu.SemaphoreType.DMA((2,)),
+            pltpu.SemaphoreType.DMA((2,)),
+            pltpu.SemaphoreType.DMA((1,)),
+            pltpu.SemaphoreType.DMA((1,)),
+            pltpu.SemaphoreType.DMA((3,)),
+            pltpu.SemaphoreType.DMA((3,)),
+            pltpu.SemaphoreType.DMA((2, NZ)),
+            pltpu.SemaphoreType.DMA((2, NZ)),
+        ],
+        compiler_params=pltpu.CompilerParams(
+            collective_id=2, has_side_effects=True, vmem_limit_bytes=32 * 1024 * 1024
+        ),
+        name="norm_and_spread",
+    )(part, own_tokens, gain)
+
+
+def pick_kernel(slot_ref, rows_ref, out_ref):
+    slots = slot_ref[0]
+    count = rows_ref.shape[0]
+    lane = lax.broadcasted_iota(jnp.int32, (slots.shape[0], count), 1)
+    chosen = jnp.where(lane == slots, 1.0, 0.0).astype(jnp.bfloat16)
+    out_ref[0] = jnp.dot(chosen, rows_ref[...], preferred_element_type=jnp.float32).astype(
+        jnp.bfloat16
+    )
+
+
+def pick(slots, rows):
+    groups, size, _ = slots.shape
+    return pl.pallas_call(
+        pick_kernel,
+        grid=(groups,),
+        in_specs=[
+            pl.BlockSpec((1, size, 1), lambda i: (i, 0, 0)),
+            pl.BlockSpec(rows.shape, lambda i: (0, 0)),
+        ],
+        out_shape=jax.ShapeDtypeStruct((groups, size, rows.shape[1]), jnp.bfloat16),
+        out_specs=pl.BlockSpec((1, size, rows.shape[1]), lambda i: (i, 0, 0)),
+        name="pick",
+    )(slots, rows)
+
+
+def dispatch_kernel(sel, rows, held, own_sem, xs, xr, ys, yr, cs, cr):
+    rank, tensor = lax.axis_index("expert"), lax.axis_index("tensor")
+    y_lo, x, z, y_hi, core, far, sides, mate = corner(rank, tensor)
+    other = 1 - y_lo
+    x_peers = [(rank_of(y_lo, lax.rem(x + d, NX), z), tensor) for d in range(1, NX)]
+    greet(x_peers + [far] + sides + [mate])
+    pending = []
+    own = pltpu.make_async_copy(sel.at[y_lo, x], rows.at[tensor, y_lo, x], own_sem.at[0])
+    own.start()
+
+    def to_side(d, here, there):
+        x_s = lax.rem(x + NX - d, NX)
+        spot = rows.at[tensor, y_lo, x_s]
+        for r in range(2):
+            pending.append(send(there, spot, ys.at[d, r], yr.at[d, r], sides[r]))
+        pending.append(send(here, spot, ys.at[d, 2], yr.at[d, 2], far))
+
+    def forward(d, r, l):
+        x_s = lax.rem(x + NX - d, NX)
+        spot = rows.at[lax.rem(y_hi + r, 2) * 2 + core, lax.rem(y_lo + l, 2), x_s]
+        index = 2 * r + l
+        pending.append(send(spot, spot, cs.at[d, index], cr.at[d, index], mate))
+
+    to_side(0, sel.at[y_lo, x], sel.at[other, x])
+    for d in (2, 1, 3):
+        to = lax.rem(x + d, NX)
+        for i in range(2):
+            src = sel.at[other if i == 0 else y_lo, to]
+            dst = held.at[x] if i == 0 else rows.at[tensor, y_lo, x]
+            pending.append(send(src, dst, xs.at[d - 1, i], xr.at[d - 1, i], x_peers[d - 1]))
+    own.wait()
+    forward(0, 0, 0)
+    for d in (1, 3, 2):
+        x_s = lax.rem(x + NX - d, NX)
+        arrived(held.at[x_s], xs.at[d - 1, 0], xr.at[d - 1, 0], x_peers[d - 1])
+        arrived(rows.at[tensor, y_lo, x_s], xs.at[d - 1, 1], xr.at[d - 1, 1], x_peers[d - 1])
+        to_side(d, rows.at[tensor, y_lo, x_s], held.at[x_s])
+        forward(d, 0, 0)
+    for d in (0, 1, 3, 2):
+        x_s = lax.rem(x + NX - d, NX)
+        for r in range(2):
+            spot = rows.at[lax.rem(y_hi + r, 2) * 2 + core, other, x_s]
+            arrived(spot, ys.at[d, r], yr.at[d, r], sides[r])
+            forward(d, r, 1)
+        spot = rows.at[(1 - y_hi) * 2 + core, y_lo, x_s]
+        arrived(spot, ys.at[d, 2], yr.at[d, 2], far)
+        forward(d, 1, 0)
+    for d in range(NX):
+        x_s = lax.rem(x + NX - d, NX)
+        for r in range(2):
+            for l in range(2):
+                spot = rows.at[lax.rem(y_hi + r, 2) * 2 + 1 - core, lax.rem(y_lo + l, 2), x_s]
+                arrived(spot, cs.at[d, 2 * r + l], cr.at[d, 2 * r + l], mate)
+    for copy in pending:
+        copy.wait_send()
+
+
+def dispatch(sel):
+    any_space = pl.BlockSpec(memory_space=pl.ANY)
+    return pl.pallas_call(
+        dispatch_kernel,
+        out_shape=(
+            jax.ShapeDtypeStruct((4,) + sel.shape, sel.dtype),
+            jax.ShapeDtypeStruct(sel.shape[1:], sel.dtype),
+        ),
+        in_specs=[any_space],
+        out_specs=(any_space, any_space),
+        scratch_shapes=[
+            pltpu.SemaphoreType.DMA((1,)),
+            pltpu.SemaphoreType.DMA((NX - 1, 2)),
+            pltpu.SemaphoreType.DMA((NX - 1, 2)),
+            pltpu.SemaphoreType.DMA((NX, 3)),
+            pltpu.SemaphoreType.DMA((NX, 3)),
+            pltpu.SemaphoreType.DMA((NX, 4)),
+            pltpu.SemaphoreType.DMA((NX, 4)),
+        ],
+        compiler_params=pltpu.CompilerParams(collective_id=3, has_side_effects=True),
+        name="dispatch",
+    )(sel)[0]
+
+
+def expert_kernel(rows_ref, up_ref, down_ref, out_ref):
+    quarters, groups, size, width = rows_ref.shape
+    count = groups * size
+    units = down_ref.shape[1]
+    total = jnp.zeros((count, up_ref.shape[2]), jnp.float32)
+    for q in range(quarters):
+        total += jnp.dot(
+            rows_ref[q].reshape(count, width), up_ref[q], preferred_element_type=jnp.float32
+        )
+    gate, up = total[:, :units], total[:, units:]
+    active = (gate * jax.nn.sigmoid(1.702 * gate) * (up + 1.0)).astype(jnp.bfloat16)
+    for q in range(quarters):
+        value = jnp.dot(active, down_ref[q], preferred_element_type=jnp.float32)
+        out_ref[q] = value.astype(jnp.bfloat16).reshape(groups, size, width)
+
+
+def run_expert(rows, up, down):
+    quarters, groups, size, width = rows.shape
+    step = 2
+    block = pl.BlockSpec((quarters, step, size, width), lambda i: (0, i, 0, 0))
+    return pl.pallas_call(
+        expert_kernel,
+        grid=(groups // step,),
+        in_specs=[
+            block,
+            pl.BlockSpec(up.shape, lambda i: (0, 0, 0)),
+            pl.BlockSpec(down.shape, lambda i: (0, 0, 0)),
+        ],
+        out_shape=jax.ShapeDtypeStruct(rows.shape, jnp.bfloat16),
+        out_specs=block,
+        compiler_params=pltpu.CompilerParams(vmem_limit_bytes=48 * 1024 * 1024),
+        name="run_expert",
+    )(rows, up, down)
+
+
+def collect_kernel(part, out, mine, core_in, side_out, side_in, x_out, ms, cs, cr, ys, yr, xs, xr):
+    rank, tensor = lax.axis_index("expert"), lax.axis_index("tensor")
+    y_lo, x, z, y_hi, core, far, sides, mate = corner(rank, tensor)
+    other = 1 - y_lo
+    x_peers = [(rank_of(y_lo, lax.rem(x + d, NX), z), tensor) for d in range(1, NX)]
+    greet(x_peers + [far] + sides + [mate])
+    pending, loads = [], {}
+    order = (2, 1, 3, 0)
+    def where(kind):
+        half = y_hi if kind in (0, 3) else 1 - y_hi
+        return half, (other if kind < 2 else y_lo)
+
+    for d in order:
+        x_h = lax.rem(x + d, NX)
+        for kind in range(4):
+            half, side = where(kind)
+            src = part.at[half * 2 + 1 - core, side, x_h]
+            pending.append(
+                send(src, core_in.at[d, kind], cs.at[d, kind], cr.at[d, kind], mate)
+            )
+            load = pltpu.make_async_copy(
+                part.at[half * 2 + core, side, x_h], mine.at[d, kind], ms.at[d, kind]
+            )
+            load.start()
+            loads[d, kind] = load
+    for d in order:
+        for kind in range(4):
+            arrived(core_in.at[d, kind], cs.at[d, kind], cr.at[d, kind], mate)
+            loads[d, kind].wait()
+            both = f32(mine[d, kind]) + f32(core_in[d, kind])
+            side_out[d, kind] = both.astype(jnp.bfloat16)
+            if kind < 3:
+                to = far if kind == 2 else sides[kind]
+                pending.append(
+                    send(
+                        side_out.at[d, kind], side_in.at[d, kind], ys.at[d, kind], yr.at[d, kind], to
+                    )
+                )
+    for d in order:
+        for kind in range(3):
+            to = far if kind == 2 else sides[kind]
+            arrived(side_in.at[d, kind], ys.at[d, kind], yr.at[d, kind], to)
+            if kind == 0:
+                continue
+            first = side_in[d, 0] if kind == 1 else side_out[d, 3]
+            both = (f32(first) + f32(side_in[d, kind])).astype(jnp.bfloat16)
+            i = kind - 1
+            owner = other if kind == 1 else y_lo
+            if d == 0:
+                out[owner, x] = both
+            else:
+                x_out[d - 1, i] = both
+                pending.append(
+                    send(
+                        x_out.at[d - 1, i], out.at[owner, x], xs.at[d - 1, i], xr.at[d - 1, i],
+                        x_peers[d - 1],
+                    )
+                )
+    for d in order[:-1]:
+        x_e = lax.rem(x + NX - d, NX)
+        for i in range(2):
+            owner = other if i == 0 else y_lo
+            arrived(out.at[owner, x_e], xs.at[d - 1, i], xr.at[d - 1, i], x_peers[d - 1])
+    for copy in pending:
+        copy.wait_send()
+
+
+def collect(part):
+    piece = part.shape[3:]
+    return pl.pallas_call(
+        collect_kernel,
+        out_shape=jax.ShapeDtypeStruct(part.shape[1:], part.dtype),
+        in_specs=[pl.BlockSpec(memory_space=pl.ANY)],
+        out_specs=pl.BlockSpec(memory_space=pltpu.VMEM),
+        scratch_shapes=[
+            pltpu.VMEM((NX, 4) + piece, jnp.bfloat16),
+            pltpu.VMEM((NX, 4) + piece, jnp.bfloat16),
+            pltpu.VMEM((NX, 4) + piece, jnp.bfloat16),
+            pltpu.VMEM((NX, 3) + piece, jnp.bfloat16),
+            pltpu.VMEM((NX - 1, 2) + piece, jnp.bfloat16),
+            pltpu.SemaphoreType.DMA((NX, 4)),
+            pltpu.SemaphoreType.DMA((NX, 4)),
+            pltpu.SemaphoreType.DMA((NX, 4)),
+            pltpu.SemaphoreType.DMA((NX, 3)),
+            pltpu.SemaphoreType.DMA((NX, 3)),
+            pltpu.SemaphoreType.DMA((NX - 1, 2)),
+            pltpu.SemaphoreType.DMA((NX - 1, 2)),
+        ],
+        compiler_params=pltpu.CompilerParams(
+            collective_id=4, has_side_effects=True, vmem_limit_bytes=48 * 1024 * 1024
+        ),
+        name="collect",
+    )(part)
+
+
+def mix_kernel(slot_ref, weight_ref, rows_ref, out_ref):
+    count = out_ref.shape[1]
+    row = lax.broadcasted_iota(jnp.int32, (count, slot_ref.shape[1]), 0) + pl.program_id(0) * count
+    share = jnp.where(row == slot_ref[...], weight_ref[...], 0.0).astype(jnp.bfloat16)
+    out_ref[0] = jnp.dot(share, rows_ref[...], preferred_element_type=jnp.float32).astype(
+        jnp.bfloat16
+    )
+
+
+def mix(slots, weights, rows, blocks, count):
+    width = rows.shape[1]
+    whole = lambda i: (0, 0)
+    return pl.pallas_call(
+        mix_kernel,
+        grid=(blocks,),
+        in_specs=[
+            pl.BlockSpec(slots.shape, whole),
+            pl.BlockSpec(weights.shape, whole),
+            pl.BlockSpec(rows.shape, whole),
+        ],
+        out_shape=jax.ShapeDtypeStruct((blocks, count, width), jnp.bfloat16),
+        out_specs=pl.BlockSpec((1, count, width), lambda i: (i, 0, 0)),
+        name="mix",
+    )(slots, weights, rows)
+
+
+def home_kernel(sums, hidden, out, staged, landed, zs, zr):
+    rank, tensor = lax.axis_index("expert"), lax.axis_index("tensor")
+    y_lo, x, z = place_of(rank)
+    ring = [
+        (rank_of(y_lo, x, lax.rem(z + 1, NZ)), tensor),
+        (rank_of(y_lo, x, lax.rem(z + NZ - 1, NZ)), tensor),
+    ]
+    greet(ring)
+    rows = hidden.shape[0] // 2
+    half = NZ // 2
+    pending = []
+
+    def reach(direction, piece):
+        return half if direction == piece else half - 1
+
+    def got(direction, steps, piece):
+        index = 2 * steps + piece
+        arrived(
+            landed.at[direction, index], zs.at[direction, index], zr.at[direction, index],
+            ring[direction],
+        )
+        return f32(landed[direction, index])
+
+    for steps in range(half, 0, -1):
+        for piece in range(2):
+            for direction in range(2):
+                if steps > reach(direction, piece):
+                    continue
+                home = lax.rem(z + (steps if direction == 0 else NZ - steps), NZ)
+                mine = f32(sums[home, pl.ds(piece * rows, rows)])
+                if steps < reach(direction, piece):
+                    mine = mine + got(direction, steps, piece)
+                index = 2 * (steps - 1) + piece
+                staged[direction, index] = mine.astype(jnp.bfloat16)
+                pending.append(
+                    send(
+                        staged.at[direction, index], landed.at[direction, index],
+                        zs.at[direction, index], zr.at[direction, index], ring[direction],
+                    )
+                )
+    for piece in range(2):
+        span = pl.ds(piece * rows, rows)
+        total = f32(sums[z, span])
+        for direction in range(2):
+            total = total + got(direction, 0, piece)
+        out[span] = (f32(hidden[span]) + total).astype(jnp.bfloat16)
+    for copy in pending:
+        copy.wait_send()
+
+
+def bring_home(sums, hidden):
+    rows, width = hidden.shape
+    vmem = pl.BlockSpec(memory_space=pltpu.VMEM)
+    return pl.pallas_call(
+        home_kernel,
+        out_shape=jax.ShapeDtypeStruct(hidden.shape, hidden.dtype),
+        in_specs=[vmem, vmem],
+        out_specs=vmem,
+        scratch_shapes=[
+            pltpu.VMEM((2, NZ, rows // 2, width), jnp.bfloat16),
+            pltpu.VMEM((2, NZ, rows // 2, width), jnp.bfloat16),
+            pltpu.SemaphoreType.DMA((2, NZ)),
+            pltpu.SemaphoreType.DMA((2, NZ)),
+        ],
+        compiler_params=pltpu.CompilerParams(
+            collective_id=5, has_side_effects=True, vmem_limit_bytes=32 * 1024 * 1024
+        ),
+        name="bring_home",
+    )(sums, hidden)
+
+
+def routing_slab(routed_experts, route_weights, expert_count, capacity):
+    row_count, top_count = routed_experts.shape
+    expert_list = routed_experts.reshape(row_count * top_count)
+    one_hot = (expert_list[:, None] == jnp.arange(expert_count, dtype=jnp.int32)[None, :]).astype(
+        jnp.int32
+    )
+    earlier = jnp.cumsum(one_hot, axis=0) - one_hot
+    arrival = jnp.sum(earlier * one_hot, axis=1)
+    slot_index = expert_list * capacity + arrival
+    hit = slot_index[:, None] == jnp.arange(expert_count * capacity, dtype=jnp.int32)[None, :]
+    row = (jnp.arange(row_count * top_count, dtype=jnp.int32) // top_count + 1).astype(jnp.float32)
+    token = jnp.sum(jnp.where(hit, row[:, None], 0.0), axis=0) - 1.0
+    weight = jnp.sum(jnp.where(hit, route_weights.reshape(-1, 1), 0.0), axis=0)
+    planes = [
+        jnp.pad(
+            value.reshape(NY * NX, NZ, capacity).transpose(1, 0, 2),
+            ((0, 0), (0, 0), (0, 128 - capacity)),
+        )
+        for value in (token, weight)
+    ]
+    return jnp.concatenate(planes, axis=2)
 
 
 def key_masks(prefix_length, expert_rank, cache_rows, span, width):
@@ -354,7 +841,16 @@
     own_queries = own_queries.reshape(seq_count, head_dim, query_count)
     joined = jnp.concatenate([cache_keyval, new_key_value_rows], axis=0)[:, :, 0, :]
     joined = joined.transpose(1, 0, 2)
-    kv_all, q_all = exchange(joined, own_queries)
+    top_count = routed_experts.shape[2]
+    expert_count = lax.axis_size("expert")
+    capacity = min(row_count, max(2, 5 * row_count * top_count // (2 * expert_count)))
+    slab = routing_slab(
+        routed_experts.reshape(row_count, top_count),
+        route_weights.reshape(row_count, top_count),
+        expert_count,
+        capacity,
+    )
+    kv_all, q_all, slab_all = exchange(joined, own_queries, slab)
     mask = key_masks(prefix_length, expert_rank, cache_rows, span_dev, 2 * head_dim)
     my_x = place_of(expert_rank)[1].astype(jnp.int32).reshape(1)
     part, stat = attend(my_x, q_all, kv_all, mask)
@@ -368,67 +864,40 @@
         .transpose(3, 0, 2, 1)
         .reshape(row_count, query_cols)
     )
-    projected = jnp.dot(attended, w_out, preferred_element_type=jnp.float32)
-    own_cols = lax.dynamic_slice_in_dim(
-        projected, tensor_rank * quarter, quarter, 1
-    ) + tokens.reshape(row_count, quarter).astype(jnp.float32)
-    residual_term = lax.dynamic_update_slice_in_dim(projected, own_cols, tensor_rank * quarter, 1)
-    hidden_sum = lax.psum(residual_term.astype(jnp.bfloat16), "tensor")
-    hidden_wide = lax.optimization_barrier(hidden_sum).astype(jnp.float32)
-    second_root = lax.rsqrt(jnp.sum(hidden_wide * hidden_wide, axis=1) / model_width + EPSILON)
-    normed = (hidden_wide * second_root[:, None] * expert_gain).astype(jnp.bfloat16)
-    top_count = routed_experts.shape[2]
-    expert_count = lax.axis_size("expert")
-    capacity = min(row_count, max(2, 5 * row_count * top_count // (2 * expert_count)))
-    expert_list = routed_experts.reshape(row_count * top_count)
-    one_hot = (expert_list[:, None] == jnp.arange(expert_count, dtype=jnp.int32)[None, :]).astype(
-        jnp.int32
-    )
-    earlier = jnp.cumsum(one_hot, axis=0) - one_hot
-    arrival = jnp.sum(earlier * one_hot, axis=1)
-    slot_index = expert_list * capacity + arrival
+    quarters = model_width // quarter
+    projected = jnp.einsum(
+        "rk,kqn->qrn",
+        attended,
+        w_out.reshape(query_cols, quarters, quarter),
+        preferred_element_type=jnp.float32,
+    ).astype(jnp.bfloat16)
+    gain = lax.dynamic_slice_in_dim(expert_gain, tensor_rank * quarter, quarter, 0)
+    hidden, spread = norm_and_spread(
+        projected, tokens.reshape(row_count, quarter), gain.reshape(1, quarter), model_width
+    )
+    token = slab_all[:, :, :capacity].astype(jnp.int32)
+    first = jnp.arange(NZ, dtype=jnp.int32)[:, None, None] * row_count
+    slot_token = jnp.where(token >= 0, token + first, -1).transpose(1, 0, 2)
+    slot_weight = slab_all[:, :, 128 : 128 + capacity].transpose(1, 0, 2)
+    groups, size = NY * NX, NZ * capacity
+    sel = pick(slot_token.reshape(groups, size, 1), spread.reshape(NZ * row_count, quarter))
+    rows = dispatch(sel.reshape(NY, NX, size, quarter))
     ffn_local = w_down.shape[1]
-    gate_up_rows = w_gate_up[0].reshape(model_width, 2 * ffn_local)
-    outgoing = (
-        jnp.zeros((expert_count * capacity, model_width), jnp.bfloat16)
-        .at[slot_index]
-        .set(jnp.repeat(normed, top_count, axis=0))
-    )
-    received = lax.all_to_all(
-        outgoing.reshape(expert_count, capacity, model_width),
-        "expert",
-        split_axis=0,
-        concat_axis=0,
-        tiled=True,
-    )
-    gate_up = jnp.dot(
-        received.reshape(expert_count * capacity, model_width),
-        gate_up_rows,
-        preferred_element_type=jnp.float32,
-    )
-    gate_part = gate_up[:, :ffn_local]
-    up_part = gate_up[:, ffn_local:]
-    activated = (gate_part * jax.nn.sigmoid(1.702 * gate_part) * (up_part + 1.0)).astype(
-        jnp.bfloat16
-    )
-    partial_value = jnp.dot(activated, w_down[0], preferred_element_type=jnp.float32)
-    weight_cols = route_weights.reshape(row_count, top_count, 1)
-    owner_sums = lax.psum_scatter(
-        partial_value.astype(jnp.bfloat16), "tensor", scatter_dimension=1, tiled=True
-    ).astype(jnp.float32)
-    returned_rows = lax.all_to_all(
-        owner_sums.reshape(expert_count, capacity, quarter).astype(jnp.bfloat16),
-        "expert",
-        split_axis=0,
-        concat_axis=0,
-        tiled=True,
-    ).astype(jnp.float32)
-    picked = returned_rows.reshape(expert_count * capacity, quarter)[slot_index]
-    expert_mix = jnp.sum(picked.reshape(row_count, top_count, quarter) * weight_cols, axis=1)
-    hidden_quarter = lax.dynamic_slice_in_dim(hidden_wide, tensor_rank * quarter, quarter, 1)
-    layer_output = (
-        (hidden_quarter + expert_mix).astype(jnp.bfloat16).reshape(span_dev, seq_count, quarter)
-    )
+    units = -(-ffn_local // 128) * 128
+    up = jnp.pad(w_gate_up[0], ((0, 0), (0, 0), (0, units - ffn_local)))
+    up = up.reshape(quarters, quarter, 2 * units)
+    down = jnp.pad(w_down[0], ((0, units - ffn_local), (0, 0)))
+    down = down.reshape(units, quarters, quarter).transpose(1, 0, 2)
+    value = run_expert(rows.reshape(quarters, groups, size, quarter), up, down)
+    returned = collect(value.reshape(quarters, NY, NX, size, quarter))
+    sums = mix(
+        slot_token.reshape(1, groups * size),
+        slot_weight.reshape(1, groups * size),
+        returned.reshape(groups * size, quarter),
+        NZ,
+        row_count,
+    )
+    layer_output = bring_home(sums, hidden).reshape(span_dev, seq_count, quarter)
     return (layer_output, new_key_value_rows)
 
 

time: 659 us -> 409 us (0.62)
  blocking collectives: 227 us -> 13.9 us
  Pallas kernels: 75.7 us -> 278 us
  waiting for transfers between devices: 170 us -> 0 us
  matrix products: 23.5 us -> 6.46 us
  between operations: 14.8 us -> 1.28 us
  other arithmetic: 30.3 us -> 18.3 us
  starting transfers between devices: 11.7 us -> 0 us
  local copies, waits for them, and re-layouts: 96.6 us -> 87.1 us
    all_to_all x1 -> x0, blocking collectives: 213 us -> none  [on_device(): lax.all_to_all(outgoing.reshape(expert_count, capacity, model_width), 'ex...]
    pallas_call x0 -> x7, Pallas kernels: none -> 202 us  [the longest x1 60.9 us: dispatch(): pl.pallas_call(dispatch_kernel, out_shape=(jax.ShapeDtypeStruct((4,) + se...]
    reduce_scatter x1 -> x0, waiting for transfers between devices: 72.2 us -> none  [on_device(): lax.psum_scatter(partial_value.astype(jnp.bfloat16), 'tensor', scatter_di...]
    all_to_all x1 -> x0, waiting for transfers between devices: 54.2 us -> none  [on_device(): lax.all_to_all(owner_sums.reshape(expert_count, capacity, quarter).astype...]
    psum x1 -> x0, waiting for transfers between devices: 44 us -> none  [on_device(): hidden_sum = lax.psum(residual_term.astype(jnp.bfloat16), 'tensor')]
    dot_general x3 -> x1, matrix products: 18.9 us -> 1.83 us  [on_device(): jnp.einsum('rk,kqn->qrn', attended, w_out.reshape(query_cols, quarters, q...]
    unnamed x45 -> x70, local copies, waits for them, and re-layouts: 6.2 us -> 20.6 us
    all_to_all x1 -> x0, starting transfers between devices: 11.6 us -> none  [on_device(): lax.all_to_all(owner_sums.reshape(expert_count, capacity, quarter).astype...]
  transfers between devices with their start and end apart: 3 -> 0, of which waited for: 3 -> 0; matrix products, arithmetic and copies ran while one was open for 1% -> 0% of each run, Pallas kernels for 0% -> 0%
where the time goes in v2:
time: 409 us; the launch traced here: 405 us
  Pallas kernels  278 us (68%)
  local copies, waits for them, and re-layouts  87.1 us (21%)
  other arithmetic  18.3 us (4%)
  blocking collectives  13.9 us (3%)
  matrix products  6.46 us (2%)
    pallas_call x1, Pallas kernels, dispatch(): pl.pallas_call(dispatch_kernel, out_shape=(jax.ShapeDtypeStruct((4,) + se...  60.9 us
    pallas_call x1, Pallas kernels, collect(): pl.pallas_call(collect_kernel, out_shape=jax.ShapeDtypeStruct(part.shape[...  49.4 us
    pallas_call x1, Pallas kernels, norm_and_spread(): pl.pallas_call(functools.partial(norm_kernel, model_width), out_shape=(ja...  35.8 us
    pallas_call x1, Pallas kernels, exchange(): pl.pallas_call(exchange_kernel, out_shape=(jax.ShapeDtypeStruct((NY * NZ,...  33.7 us
    pallas_call x1, Pallas kernels, attend(): pl.pallas_call(attend_kernel, grid=(seqs, nx), in_specs=[pl.BlockSpec(mem...  33.2 us
    pallas_call x1, Pallas kernels, bring_home(): pl.pallas_call(home_kernel, out_shape=jax.ShapeDtypeStruct(hidden.shape,...  21.8 us
    unnamed x70, local copies, waits for them, and re-layouts  20.6 us
    reshape x2, local copies, waits for them, and re-layouts, on_device(): up = up.reshape(quarters, quarter, 2 * units)  20.4 us

profile of v2, /device:TPU:40, one launch (start us, length us, event | category | flops | bytes accessed | tf_op | source)
XLA Modules:
  0.0 405.0 jit_solution(12057943306017389063)
XLA Ops:
  18.5 13.9 %all_gather.3 = bf16[64,2,2880]{0,1,2:T(2,128)(2,1)} all-gather(bf16[64,2,720]{0,1,2:T(2,128)(2,1)S(1)} %copy.178), channel_id=1, replica_groups=mesh['expert'=64,'tensor'=4] {'tensor'}, dimensions={2}, use_global_device_ids=true | all-gather | bytes 921600 | tf_op jit(solution)/shard_map/all_gather | solution.py:808
  32.4 4.2 %copy.179 = bf16[64,2,2880]{2,0,1:T(8,128)(2,1)} copy(bf16[64,2,2880]{0,1,2:T(2,128)(2,1)} %all_gather.3) | data formatting | bytes 1474560 | tf_op jit(solution)/shard_map/all_gather | solution.py:808
  39.2 2.8 copy.180
  42.0 2.9 convert_element_type.86
  48.8 3.0 copy.190
  51.8 3.2 reshape.360
  55.0 2.9 convolution_multiply_fusion
  66.1 2.6 select_convert_fusion.mask_ref
  68.8 4.1 %copy.210 = bf16[1,360,2880]{1,2,0:T(8,128)(2,1)} copy(bf16[1,360,2880]{2,1,0:T(8,128)(2,1)} %param.23) | data formatting | bytes 4147200 | tf_op args[11]
  72.9 3.2 pad.18
  76.1 4.2 %copy.211 = bf16[384,4,720]{2,0,1:T(8,128)(2,1)} copy(bf16[384,4,720]{0,2,1:T(8,128)(2,1)} %bitcast.89) | data formatting | bytes 4423680 | tf_op jit(solution)/shard_map/reshape | solution.py:890
  80.3 33.7 %exchange.1 = (bf16[16,2,256,128]{3,2,1,0:T(8,128)(2,1)}, bf16[4,2,64,512]{3,2,1,0:T(8,128)(2,1)}, f32[8,8,256]{2,1,0:T(8,128)}) custom-call(bf16[2,256,128]{2,1,0:T(8,128)(2,1)} %maximum_bitcast_fusion.kv, bf16[2,64,512]{2,1,0:T(8,128)(2,1)} %reshape.341.q, f32[8,8,256]{2,1,0:T(8,128)} %select_maximum_fusion.slab), custom_call_target="tpu_custom_call" | custom-call | tf_op jit(solution)/shard_map/exchange/pallas_call | solution.py:129
  118.2 33.2 %attend.1 = (bf16[4,2,64,512]{3,2,1,0:T(8,128)(2,1)S(1)}, f32[4,2,8,512]{3,2,1,0:T(8,128)S(1)}) custom-call(s32[1]{0:T(128)} %bitcast.16.my_x, bf16[4,2,64,512]{3,2,1,0:T(8,128)(2,1)S(1)} %copy-done.8, bf16[16,2,256,128]{3,2,1,0:T(8,128)(2,1)S(1)} %copy-done.6, bf16[2,16,256,128]{3,2,1,0:T(8,128)(2,1)S(1)} %copy-done.3), custom_call_target="tpu_custom_call" | custom-call | tf_op jit(solution)/shard_map/attend/pallas_call | solution.py:207
  152.8 9.3 %send_back.1 = (bf16[4,2,64,512]{3,2,1,0:T(8,128)(2,1)}, f32[4,2,8,512]{3,2,1,0:T(8,128)}) custom-call(bf16[4,2,64,512]{3,2,1,0:T(8,128)(2,1)} %copy-done.9, f32[4,2,8,512]{3,2,1,0:T(8,128)} %copy-done.10), custom_call_target="tpu_custom_call" | custom-call | tf_op jit(solution)/shard_map/send_back/pallas_call | solution.py:260
  173.5 35.8 %norm_and_spread.1 = (bf16[128,720]{1,0:T(8,128)(2,1)S(1)}, bf16[8,128,720]{2,1,0:T(8,128)(2,1)S(1)}) custom-call(bf16[4,128,720]{2,1,0:T(8,128)(2,1)S(1)} %bitcast.86, bf16[128,720]{1,0:T(8,128)(2,1)S(1)} %reshape.350.own_tokens, f32[1,720]{1,0:T(1,128)S(1)} %reshape.351.gain), custom_call_target="tpu_custom_call" | custom-call | tf_op jit(solution)/shard_map/norm_and_spread/pallas_call | solution.py:362
  210.5 7.7 %pick.1 = bf16[8,160,720]{2,1,0:T(8,128)(2,1)} custom-call(s32[8,160,1]{2,1,0:T(8,128)} %reshape.362.slot_ref, bf16[1024,720]{1,0:T(8,128)(2,1)} %bitcast.87), custom_call_target="tpu_custom_call" | custom-call | tf_op jit(solution)/shard_map/pick/pallas_call | solution.py:405
  218.1 4.6 %pad.17 = bf16[2880,2,384]{0,2,1:T(8,128)(2,1)} pad(bf16[2880,2,360]{0,2,1:T(8,128)(2,1)} %bitcast.93, bf16[]{:T(256)} %constant.148.clone.1), padding=0_0x0_0x0_24 | pad | bytes 8570882 | tf_op jit(solution)/shard_map/jit(_pad)/pad | solution.py:887
  222.8 11.8 %reshape.364 = bf16[4,720,768]{1,0,2:T(4,128)(2,1)} reshape(bf16[2880,2,384]{0,2,1:T(8,128)(2,1)} %pad.17) | data formatting | bytes 8847360 | tf_op jit(solution)/shard_map/reshape | solution.py:888
  234.6 8.6 %copy.213.up_ref = bf16[4,720,768]{2,1,0:T(8,128)(2,1)} copy(bf16[4,720,768]{1,0,2:T(4,128)(2,1)} %reshape.364) | data formatting | bytes 8847360 | tf_op jit(solution)/shard_map/reshape | solution.py:888
  243.1 60.9 %dispatch.1 = (bf16[4,2,4,160,720]{4,3,2,1,0:T(8,128)(2,1)}, bf16[4,160,720]{2,1,0:T(8,128)(2,1)}) custom-call(bf16[2,4,160,720]{3,2,1,0:T(8,128)(2,1)} %bitcast.91), custom_call_target="tpu_custom_call" | custom-call | tf_op jit(solution)/shard_map/dispatch/pallas_call | solution.py:477
  304.1 19.6 %run_expert.1 = bf16[4,8,160,720]{3,2,1,0:T(8,128)(2,1)} custom-call(bf16[4,8,160,720]{3,2,1,0:T(8,128)(2,1)} %bitcast.92, bf16[4,720,768]{2,1,0:T(8,128)(2,1)} %copy.213.up_ref, bf16[4,384,720]{2,1,0:T(8,128)(2,1)S(1)} %bitcast.84), custom_call_target="tpu_custom_call" | custom-call | tf_op jit(solution)/shard_map/run_expert/pallas_call | solution.py:519
  323.7 49.4 %collect.1 = bf16[2,4,160,720]{3,2,1,0:T(8,128)(2,1)S(1)} custom-call(bf16[4,2,4,160,720]{4,3,2,1,0:T(8,128)(2,1)} %bitcast.88), custom_call_target="tpu_custom_call" | custom-call | tf_op jit(solution)/shard_map/collect/pallas_call | solution.py:603
  374.4 6.6 %mix.1.sums = bf16[8,128,720]{2,1,0:T(8,128)(2,1)} custom-call(s32[1,1280]{1,0:T(1,128)} %reshape.344.slot_ref, f32[1,1280]{1,0:T(1,128)} %reshape.345.weight_ref, bf16[1280,720]{1,0:T(8,128)(2,1)} %bitcast.85), custom_call_target="tpu_custom_call" | custom-call | tf_op jit(solution)/shard_map/mix/pallas_call | solution.py:641
  382.4 21.8 %bring_home.1 = bf16[128,720]{1,0:T(8,128)(2,1)S(1)} custom-call(bf16[8,128,720]{2,1,0:T(8,128)(2,1)S(1)} %copy-done.5, bf16[128,720]{1,0:T(8,128)(2,1)S(1)} %get-tuple-element.21.hidden), custom_call_target="tpu_custom_call" | custom-call | tf_op jit(solution)/shard_map/bring_home/pallas_call | solution.py:708
  (144 shorter events, 53.8 us)
Async XLA Ops:
  0.6 1.8 copy-start
  2.5 6.4 %copy-start.16 = (f32[32]{0:T(128)}, f32[32]{0:T(128)S(1)}, u32[]{:S(2)}) copy-start(f32[32]{0:T(128)S(1)} %multiply_exponential_fusion) | copy-start | bytes 388
  36.6 10.0 %copy-start.17 = (f32[32]{0:T(128)S(1)}, f32[32]{0:T(128)}, u32[]{:S(2)}) copy-start(f32[32]{0:T(128)} %copy-done.16) | copy-start | bytes 388
  36.6 10.6 %copy-start.11 = (bf16[192,2,1,128]{3,0,1,2:T(8,128)(2,1)S(1)}, bf16[192,2,1,128]{3,0,1,2:T(8,128)(2,1)}, u32[]{:S(2)}) copy-start(bf16[192,2,1,128]{3,0,1,2:T(8,128)(2,1)} %copy.189) | copy-start | bytes 294916
  47.1 7.9 %copy-start.15 = (f32[2880]{0:T(1024)S(1)}, f32[2880]{0:T(1024)}, u32[]{:S(2)}) copy-start(f32[2880]{0:T(1024)} %param.13) | copy-start | bytes 34564
  57.8 8.2 %copy-start.18 = (s32[2]{0:T(128)S(1)}, s32[2]{0:T(128)}, u32[]{:S(2)}) copy-start(s32[2]{0:T(128)} %param.18) | copy-start | bytes 28
  57.8 8.2 %copy-start.19 = (s32[256]{0:T(256)S(1)}, s32[256]{0:T(256)}, u32[]{:S(2)}) copy-start(s32[256]{0:T(256)} %iota_add_fusion) | copy-start | bytes 3076
  57.9 8.2 %copy-start.21 = (s32[128]{0:T(128)S(1)}, s32[128]{0:T(128)}, u32[]{:S(2)}) copy-start(s32[128]{0:T(128)} %multiply_add_fusion.2) | copy-start | bytes 1540
  57.9 8.2 %copy-start.22 = (pred[128]{0:T(512)(128)(4,1)S(1)}, pred[128]{0:T(512)(128)(4,1)}, u32[]{:S(2)}) copy-start(pred[128]{0:T(512)(128)(4,1)} %iota_compare_fusion.8) | copy-start | bytes 388
  57.9 8.2 %copy-start.23 = (pred[256]{0:T(512)(128)(4,1)S(1)}, pred[256]{0:T(512)(128)(4,1)}, u32[]{:S(2)}) copy-start(pred[256]{0:T(512)(128)(4,1)} %iota_compare_fusion.6) | copy-start | bytes 772
  57.9 8.2 %copy-start.24 = (s32[16]{0:T(128)S(1)}, s32[16]{0:T(128)}, u32[]{:S(2)}) copy-start(s32[16]{0:T(128)} %get-tuple-element.54) | copy-start | bytes 196
  57.9 8.2 %copy-start.25 = (s32[16]{0:T(128)S(1)}, s32[16]{0:T(128)}, u32[]{:S(2)}) copy-start(s32[16]{0:T(128)} %get-tuple-element.55) | copy-start | bytes 196
  57.9 8.2 %copy-start.26 = (s32[16]{0:T(128)S(1)}, s32[16]{0:T(128)}, u32[]{:S(2)}) copy-start(s32[16]{0:T(128)} %get-tuple-element.52) | copy-start | bytes 196
  57.9 8.2 %copy-start.27 = (s32[16]{0:T(128)S(1)}, s32[16]{0:T(128)}, u32[]{:S(2)}) copy-start(s32[16]{0:T(128)} %get-tuple-element.53) | copy-start | bytes 196
  57.9 8.2 %copy-start.28 = (pred[16]{0:T(512)(128)(4,1)S(1)}, pred[16]{0:T(512)(128)(4,1)}, u32[]{:S(2)}) copy-start(pred[16]{0:T(512)(128)(4,1)} %get-tuple-element.50) | copy-start | bytes 52
  57.9 8.2 %copy-start.29 = (pred[16]{0:T(512)(128)(4,1)S(1)}, pred[16]{0:T(512)(128)(4,1)}, u32[]{:S(2)}) copy-start(pred[16]{0:T(512)(128)(4,1)} %get-tuple-element.51) | copy-start | bytes 52
  57.9 8.2 %copy-start.30 = (pred[128]{0:T(512)(128)(4,1)S(1)}, pred[128]{0:T(512)(128)(4,1)}, u32[]{:S(2)}) copy-start(pred[128]{0:T(512)(128)(4,1)} %get-tuple-element.48) | copy-start | bytes 388
  58.0 8.2 %copy-start.31 = (pred[128]{0:T(512)(128)(4,1)S(1)}, pred[128]{0:T(512)(128)(4,1)}, u32[]{:S(2)}) copy-start(pred[128]{0:T(512)(128)(4,1)} %get-tuple-element.49) | copy-start | bytes 388
  114.0 1.6 copy-start.3
  118.2 47.2 %copy-start.14 = (f32[8,8,256]{2,1,0:T(8,128)S(1)}, f32[8,8,256]{2,1,0:T(8,128)}, u32[]{:S(2)}) copy-start(f32[8,8,256]{2,1,0:T(8,128)} %get-tuple-element.12) | copy-start | bytes 196612
  118.2 47.2 %copy-start.20 = (s32[8]{0:T(128)S(1)}, s32[8]{0:T(128)}, u32[]{:S(2)}) copy-start(s32[8]{0:T(128)} %iota_multiply_fusion) | copy-start | bytes 100
  168.1 4.4 %copy-start.13 = (s32[8,8,20]{2,1,0:T(8,128)S(1)}, s32[8,8,20]{2,1,0:T(8,128)}, u32[]{:S(2)}) copy-start(s32[8,8,20]{2,1,0:T(8,128)} %copy-done.12) | copy-start | bytes 15364
  234.5 69.5 %copy-start.2 = (bf16[384,4,720]{2,0,1:T(8,128)(2,1)S(1)}, bf16[384,4,720]{2,0,1:T(8,128)(2,1)}, u32[]{:S(2)}) copy-start(bf16[384,4,720]{2,0,1:T(8,128)(2,1)} %copy.211) | copy-start | bytes 6635524
  374.4 30.6 %copy-start.1 = (bf16[512,2880]{0,1:T(8,128)(2,1)S(1)}, bf16[512,2880]{0,1:T(8,128)(2,1)}, u32[]{:S(2)}) copy-start(bf16[512,2880]{0,1:T(8,128)(2,1)} %param.16) | copy-start | bytes 8847364
  (8 other events, 8.7 us)

commit v3 on v2

v3 whole, which is shorter than its diff:
```python
import functools
import math

import jax
import jax.numpy as jnp
from jax import lax
from jax.experimental import pallas as pl
from jax.experimental.pallas import tpu as pltpu
from jax.sharding import PartitionSpec as P

EPSILON = 1e-05
ROPE_BASE = 150000.0
NEG = -1e30
MESH = pl.DeviceIdType.MESH
NY, NX, NZ = 2, 4, 8
LOG2E = 1.4426950408889634


def place_of(expert_rank):
    return expert_rank // (NX * NZ), (expert_rank // NZ) % NX, expert_rank % NZ


def rank_of(y_lo, x, z):
    return (y_lo * NX + x) * NZ + z


def greet(devices):
    barrier = pltpu.get_barrier_semaphore()
    for device in devices:
        pl.semaphore_signal(barrier, inc=1, device_id=device, device_id_type=MESH)
    pl.semaphore_wait(barrier, len(devices))


def send(src, dst, send_sem, recv_sem, device):
    copy = pltpu.make_async_remote_copy(
        src_ref=src,
        dst_ref=dst,
        send_sem=send_sem,
        recv_sem=recv_sem,
        device_id=device,
        device_id_type=MESH,
    )
    copy.start()
    return copy


def arrived(dst, send_sem, recv_sem, device):
    pltpu.make_async_remote_copy(
        src_ref=dst,
        dst_ref=dst,
        send_sem=send_sem,
        recv_sem=recv_sem,
        device_id=device,
        device_id_type=MESH,
    ).wait_recv()


def swap_blocks(value):
    half = value.shape[0] // 2
    top, bottom = value[:half], value[half:]
    left = lax.broadcasted_iota(jnp.int32, top.shape, 1) < half
    return jnp.concatenate(
        [
            jnp.where(left, top, pltpu.roll(bottom, half, 1)),
            jnp.where(left, pltpu.roll(top, half, 1), bottom),
        ],
        axis=0,
    )


def turn(first, second, cosine, sine):
    return first * cosine - second * sine, second * cosine + first * sine


def front_kernel(
    scale, own_tokens, gain, w_query, w_keyval, cosine, sine, cache, slab,
    fresh, kv_all, q_all, slab_all,
    gathered, q_own, own_sem, gs, gr, xs, xr, ys, yr, zs, zr, ts, tr,
):
    rank, tensor = lax.axis_index("expert"), lax.axis_index("tensor")
    y_lo, x, z, y_hi, core, far, sides, mate = corner(rank, tensor)
    other = 1 - y_lo
    rows, quarter = own_tokens.shape
    cache_rows, head = cache.shape[1], fresh.shape[2] // 2
    span = fresh.shape[1]
    x_peers = [(rank_of(y_lo, lax.rem(x + d, NX), z), tensor) for d in range(1, NX)]
    y_peer = (rank_of(other, x, z), tensor)
    z_peers = [(rank_of(y_lo, x, lax.rem(z + d, NZ)), tensor) for d in range(1, NZ)]
    ring = [z_peers[0], z_peers[-1]]
    greet(x_peers + [y_peer] + z_peers + [far, mate])
    pending = []
    parts = (pl.ds(0, cache_rows), pl.ds(cache_rows, span))
    first = (cache, fresh)

    def slot(part, direction, steps, piece):
        origin = lax.rem(z + (NZ - steps if direction == 0 else steps), NZ)
        return kv_all.at[origin * 2 + (y_lo if piece == 0 else other), :, parts[part]]

    def sems(part, direction, step, piece):
        index = 2 * (step - 1) + piece
        return zs.at[part, direction, index], zr.at[part, direction, index]

    def pass_on(part, direction, step, piece):
        block = slot(part, direction, step - 1, piece)
        src = first[part] if step == 1 and piece == 0 else block
        pending.append(send(src, block, *sems(part, direction, step, piece), ring[direction]))

    def got(part, direction, step, piece):
        arrived(
            slot(part, direction, step, piece), *sems(part, direction, step, piece), ring[direction]
        )

    def begin(part):
        block = slot(part, 0, 0, 0)
        copy = pltpu.make_async_copy(first[part], block, own_sem.at[part])
        copy.start()
        pending.append(send(first[part], block, ys.at[part], yr.at[part], y_peer))
        for direction in range(2):
            pass_on(part, direction, 1, 0)
        return copy

    def begin_other(part):
        arrived(slot(part, 0, 0, 1), ys.at[part], yr.at[part], y_peer)
        for direction in range(2):
            pass_on(part, direction, 1, 1)

    half = NZ // 2

    def step_on(part, step):
        for piece in range(2):
            for direction in range(2):
                got(part, direction, step - 1, piece)
                if step < half or direction == piece:
                    pass_on(part, direction, step, piece)

    mine = gathered.at[tensor]
    pending.append(send(own_tokens, mine, gs.at[0], gr.at[0], far))
    pending.append(send(own_tokens, mine, gs.at[1], gr.at[1], mate))
    own = [begin(0), pltpu.make_async_copy(slab.at[z], slab_all.at[z], own_sem.at[2])]
    own[1].start()
    for d in range(1, NZ):
        to = lax.rem(z + d, NZ)
        pending.append(
            send(slab.at[to], slab_all.at[z], ts.at[d - 1], tr.at[d - 1], z_peers[d - 1])
        )
    far_index, mate_index = (1 - y_hi) * 2 + core, y_hi * 2 + 1 - core
    cross_index = (1 - y_hi) * 2 + 1 - core

    def project(index, block):
        wide = f32(block)
        scaled = (wide * gain[index]).astype(jnp.bfloat16)
        span_of = pl.ds(pl.multiple_of(index * quarter, 16), quarter)
        return (
            jnp.dot(scaled, w_query[span_of, :], preferred_element_type=jnp.float32),
            jnp.dot(scaled, w_keyval[span_of, :], preferred_element_type=jnp.float32),
            jnp.sum(wide * wide, axis=1, keepdims=True),
        )

    total = project(tensor, own_tokens[...])
    begin_other(0)
    arrived(gathered.at[far_index], gs.at[0], gr.at[0], far)
    block = gathered.at[far_index]
    pending.append(send(block, block, gs.at[2], gr.at[2], mate))
    total = [a + b for a, b in zip(total, project(far_index, gathered[far_index]))]
    arrived(gathered.at[mate_index], gs.at[1], gr.at[1], mate)
    total = [a + b for a, b in zip(total, project(mate_index, gathered[mate_index]))]
    step_on(0, 2)
    arrived(gathered.at[cross_index], gs.at[2], gr.at[2], mate)
    total = [a + b for a, b in zip(total, project(cross_index, gathered[cross_index]))]
    root = lax.rsqrt(total[2] / (4 * quarter) + EPSILON)
    cos, sin = cosine[...], sine[...]
    flipped = (total[1] * root).T
    keys = turn(flipped[: head // 2], flipped[head // 2 : head], cos, sin)
    whole = jnp.concatenate([keys[0], keys[1], flipped[head:]], axis=0).T
    fresh[...] = whole.astype(jnp.bfloat16).reshape(fresh.shape)
    own.append(begin(1))
    raw = total[0] * root
    width = 2 * head
    for j in range(raw.shape[1] // width):
        pair = raw[:, j * width : (j + 1) * width].T
        turned = []
        for h in range(2):
            block = pair[h * head : (h + 1) * head]
            turned += turn(block[: head // 2], block[head // 2 :], cos, sin)
        sides_first = swap_blocks(jnp.concatenate(turned, axis=0) * scale).astype(jnp.bfloat16)
        for s in range(2):
            q_own[s, :, j * width : (j + 1) * width] = sides_first[s * head : (s + 1) * head]
    copy = pltpu.make_async_copy(q_own, q_all.at[x], own_sem.at[3])
    copy.start()
    own.append(copy)
    for d in range(1, NX):
        pending.append(send(q_own, q_all.at[x], xs.at[d - 1], xr.at[d - 1], x_peers[d - 1]))
    begin_other(1)
    step_on(0, 3)
    step_on(1, 2)
    step_on(0, 4)
    step_on(1, 3)
    step_on(1, 4)
    for part in range(2):
        for direction in range(2):
            got(part, direction, half, direction)
    for d in range(1, NX):
        arrived(q_all.at[lax.rem(x + NX - d, NX)], xs.at[d - 1], xr.at[d - 1], x_peers[d - 1])
    for d in range(1, NZ):
        arrived(
            slab_all.at[lax.rem(z + NZ - d, NZ)], ts.at[d - 1], tr.at[d - 1], z_peers[d - 1]
        )
    for copy in own:
        copy.wait()
    for copy in pending:
        copy.wait_send()


def front(scale, own_tokens, gain, w_query, w_keyval, cosine, sine, cache, slab):
    seqs, cache_rows, width = cache.shape
    rows, quarter = own_tokens.shape
    span, cols = rows // seqs, w_query.shape[1] * rows // seqs // (width // 2)
    vmem = pl.BlockSpec(memory_space=pltpu.VMEM)
    any_space = pl.BlockSpec(memory_space=pl.ANY)
    return pl.pallas_call(
        functools.partial(front_kernel, scale),
        out_shape=(
            jax.ShapeDtypeStruct((seqs, span, width), jnp.bfloat16),
            jax.ShapeDtypeStruct((NY * NZ, seqs, cache_rows + span, width), jnp.bfloat16),
            jax.ShapeDtypeStruct((NX, seqs, width // 2, cols), jnp.bfloat16),
            jax.ShapeDtypeStruct(slab.shape, slab.dtype),
        ),
        in_specs=[vmem] * 6 + [any_space] * 2,
        out_specs=(vmem, any_space, any_space, any_space),
        scratch_shapes=[
            pltpu.VMEM((4, rows, quarter), jnp.bfloat16),
            pltpu.VMEM((seqs, width // 2, cols), jnp.bfloat16),
            pltpu.SemaphoreType.DMA((4,)),
            pltpu.SemaphoreType.DMA((3,)),
            pltpu.SemaphoreType.DMA((3,)),
            pltpu.SemaphoreType.DMA((NX - 1,)),
            pltpu.SemaphoreType.DMA((NX - 1,)),
            pltpu.SemaphoreType.DMA((2,)),
            pltpu.SemaphoreType.DMA((2,)),
            pltpu.SemaphoreType.DMA((2, 2, NZ)),
            pltpu.SemaphoreType.DMA((2, 2, NZ)),
            pltpu.SemaphoreType.DMA((NZ - 1,)),
            pltpu.SemaphoreType.DMA((NZ - 1,)),
        ],
        compiler_params=pltpu.CompilerParams(
            collective_id=0, has_side_effects=True, vmem_limit_bytes=32 * 1024 * 1024
        ),
        name="front",
    )(own_tokens, gain, w_query, w_keyval, cosine, sine, cache, slab)


def attend_kernel(cache_rows, place, q_ref, kv_ref, o_ref, stat_ref, vt_ref, qa_ref, mask_ref):
    xq = pl.program_id(1)
    prefix = place[pl.program_id(0)]
    my_rank = place[place.shape[0] - 1]
    y_lo, x, z = place_of(my_rank)
    chunks, _, chunk = vt_ref.shape
    shards, _, keys, width = kv_ref.shape
    per = chunk // keys
    head, cols = q_ref.shape[2:]

    @pl.when(xq == 0)
    def _():
        for j in range(chunks):
            rows = kv_ref[j * per : (j + 1) * per, 0].reshape(chunk, width)
            flipped = rows.astype(jnp.float32).T
            vt_ref[j, :16, :] = jnp.ones((16, chunk), jnp.bfloat16)
            vt_ref[j, 16:, :] = flipped[head:].astype(jnp.bfloat16)
        span = keys - cache_rows
        old_row = lax.broadcasted_iota(jnp.int32, (cache_rows, width), 0)
        old_col = lax.broadcasted_iota(jnp.int32, (cache_rows, width), 1)
        new_row = lax.broadcasted_iota(jnp.int32, (span, width), 0)
        new_col = lax.broadcasted_iota(jnp.int32, (span, width), 1)
        old_row = jnp.where(old_col == span + NX, old_row, -1)
        in_block = (new_col >= span) & (new_col < span + NX)
        query_rank = rank_of(y_lo, new_col - span, z)
        later = (new_col < span) & (new_row > new_col)
        for j in range(shards):
            key_rank = rank_of(j % 2, x, j // 2)
            valid = jnp.maximum(prefix - key_rank * cache_rows, 0)
            beyond = jnp.where(old_row >= valid, NEG, 0.0)
            mask_ref[j, :cache_rows, :] = beyond.astype(jnp.bfloat16)
            same = jnp.where(key_rank == my_rank, 1, 0)
            hidden_key = (in_block & (key_rank > query_rank)) | (later & (same > 0))
            mask_ref[j, cache_rows:, :] = jnp.where(hidden_key, NEG, 0.0).astype(jnp.bfloat16)

    qa_ref[:head, :] = q_ref[0, 0]
    qa_ref[head:width, :] = jnp.zeros((width - head, cols), jnp.bfloat16)
    row = lax.broadcasted_iota(jnp.int32, (width, cols), 0)
    lane = lax.broadcasted_iota(jnp.int32, (width, cols), 1)
    span = head
    tri = jnp.where(xq == x, lane % span, -1)
    hot = (row == tri) | (row == span + xq) | (row == span + NX)
    qa_ref[width:, :] = jnp.where(hot, 1.0, 0.0).astype(jnp.bfloat16)
    qa = qa_ref[...]
    top = jnp.full((1, cols), -3e38, jnp.float32)
    acc = jnp.zeros((vt_ref.shape[1], cols), jnp.float32)
    for j in range(chunks):
        lhs = jnp.concatenate(
            [
                kv_ref[j * per : (j + 1) * per, 0].reshape(chunk, width),
                mask_ref[j * per : (j + 1) * per].reshape(chunk, width),
            ],
            axis=1,
        )
        scores = jnp.dot(lhs, qa, preferred_element_type=jnp.float32)
        new_top = jnp.maximum(top, jnp.max(scores, axis=0, keepdims=True))
        probs = jnp.exp2(scores - new_top).astype(jnp.bfloat16)
        acc = acc * jnp.exp2(top - new_top) + jnp.dot(
            vt_ref[j], probs, preferred_element_type=jnp.float32
        )
        top = new_top
    total = acc[0:1]
    o_ref[0, 0] = (acc[16:] / total).astype(jnp.bfloat16)
    stat_ref[0, 0, 0:1, :] = top
    stat_ref[0, 0, 1:2, :] = total
    stat_ref[0, 0, 2:, :] = jnp.zeros((6, cols), jnp.float32)


def attend(place, q_all, kv_all, cache_rows):
    nx, seqs, head, cols = q_all.shape
    shards, _, keys, width = kv_all.shape
    chunk = 2 * keys
    chunks = shards * keys // chunk
    return pl.pallas_call(
        functools.partial(attend_kernel, cache_rows),
        grid=(seqs, nx),
        in_specs=[
            pl.BlockSpec(memory_space=pltpu.SMEM),
            pl.BlockSpec((1, 1, head, cols), lambda s, i: (i, s, 0, 0)),
            pl.BlockSpec((shards, 1, keys, width), lambda s, i: (0, s, 0, 0)),
        ],
        out_shape=(
            jax.ShapeDtypeStruct((nx, seqs, head, cols), jnp.bfloat16),
            jax.ShapeDtypeStruct((nx, seqs, 8, cols), jnp.float32),
        ),
        out_specs=(
            pl.BlockSpec((1, 1, head, cols), lambda s, i: (i, s, 0, 0)),
            pl.BlockSpec((1, 1, 8, cols), lambda s, i: (i, s, 0, 0)),
        ),
        scratch_shapes=[
            pltpu.VMEM((chunks, 16 + head, chunk), jnp.bfloat16),
            pltpu.VMEM((2 * width, cols), jnp.bfloat16),
            pltpu.VMEM((shards, keys, width), jnp.bfloat16),
        ],
        compiler_params=pltpu.CompilerParams(vmem_limit_bytes=48 * 1024 * 1024),
        name="attend",
    )(place, q_all, kv_all)


def corner(rank, tensor):
    y_lo, x, z = place_of(rank)
    y_hi, core = tensor // 2, lax.rem(tensor, 2)
    far = (rank, (1 - y_hi) * 2 + core)
    sides = [(rank_of(1 - y_lo, x, z), lax.rem(y_hi + r, 2) * 2 + core) for r in range(2)]
    mate = (rank, y_hi * 2 + 1 - core)
    return y_lo, x, z, y_hi, core, far, sides, mate


def f32(value):
    return value.astype(jnp.float32)


def norm_kernel(
    model_width, o, stat, w_out, own_tokens, gain, hidden, spread,
    o_in, stat_in, to_core, core_in, core_out, far_in, squares, squares_in,
    os, orr, ss, sr, cs, cr, fs, fr, qs, qr, zs, zr,
):
    rank, tensor = lax.axis_index("expert"), lax.axis_index("tensor")
    y_lo, x, z, y_hi, core, far, sides, mate = corner(rank, tensor)
    cross = (rank, (1 - y_hi) * 2 + 1 - core)
    ring = [
        (rank_of(y_lo, x, lax.rem(z + 1, NZ)), tensor),
        (rank_of(y_lo, x, lax.rem(z + NZ - 1, NZ)), tensor),
    ]
    x_peers = [(rank_of(y_lo, lax.rem(x + d, NX), z), tensor) for d in range(1, NX)]
    greet([mate, far, cross] + ring + x_peers)
    pending = []
    for d in range(1, NX):
        to, i = lax.rem(x + d, NX), d - 1
        pending.append(send(stat.at[to], stat_in.at[i], ss.at[i], sr.at[i], x_peers[i]))
        pending.append(send(o.at[to], o_in.at[i], os.at[i], orr.at[i], x_peers[i]))
    stats, values = [stat[x]], [o[x]]
    for i in range(NX - 1):
        arrived(stat_in.at[i], ss.at[i], sr.at[i], x_peers[i])
        arrived(o_in.at[i], os.at[i], orr.at[i], x_peers[i])
        stats.append(stat_in[i])
        values.append(o_in[i])
    seqs, head, cols = values[0].shape
    merged = []
    for s in range(seqs):
        tops = [value[s, 0:1] for value in stats]
        top = functools.reduce(jnp.maximum, tops)
        shares = [jnp.exp2(a - top) * value[s, 1:2] for a, value in zip(tops, stats)]
        whole = functools.reduce(jnp.add, shares)
        merged.append(
            functools.reduce(jnp.add, [f32(v[s]) * (a / whole) for v, a in zip(values, shares)])
        )
    both = jnp.concatenate(merged, axis=0)
    wide_head = seqs * head
    attended = jnp.concatenate(
        [
            swap_blocks(both[:, j * wide_head : (j + 1) * wide_head].T)
            for j in range(cols // wide_head)
        ],
        axis=1,
    ).astype(jnp.bfloat16)
    quarter = own_tokens.shape[1]

    def projected(index):
        span_of = pl.ds(pl.multiple_of(index * quarter, 16), quarter)
        return lax.dot_general(
            attended, w_out[span_of, :], (((1,), (1,)), ((), ())),
            preferred_element_type=jnp.float32,
        )

    order = [1 - y_hi, y_hi]
    for i in range(2):
        to_core[i] = projected(order[i] * 2 + 1 - core).astype(jnp.bfloat16)
        pending.append(send(to_core.at[i], core_in.at[i], cs.at[i], cr.at[i], mate))
    for_far = projected(order[0] * 2 + core)
    arrived(core_in.at[0], cs.at[0], cr.at[0], mate)
    core_out[...] = (for_far + f32(core_in[0])).astype(jnp.bfloat16)
    pending.append(send(core_out, far_in, fs.at[0], fr.at[0], far))
    near = f32(own_tokens[...]) + projected(order[1] * 2 + core)
    arrived(core_in.at[1], cs.at[1], cr.at[1], mate)
    near = near + f32(core_in[1])
    arrived(far_in, fs.at[0], fr.at[0], far)
    rounded = (near + f32(far_in[...])).astype(jnp.bfloat16)
    hidden[...] = rounded
    wide = f32(rounded)
    own_squares = jnp.sum(wide * wide, axis=1, keepdims=True)
    squares[...] = jnp.broadcast_to(own_squares, squares.shape)
    trio = [mate, far, cross]
    for i in range(3):
        pending.append(send(squares, squares_in.at[i], qs.at[i], qr.at[i], trio[i]))
    total = own_squares
    for i in range(3):
        arrived(squares_in.at[i], qs.at[i], qr.at[i], trio[i])
        total = total + squares_in[i, :, 0:1]
    root = lax.rsqrt(total / model_width + EPSILON)
    spread[z] = (wide * root * gain[...]).astype(jnp.bfloat16)
    rows = wide.shape[0] // 2

    def slot(direction, steps, piece):
        origin = lax.rem(z + (NZ - steps if direction == 0 else steps), NZ)
        return spread.at[origin, pl.ds(piece * rows, rows)]

    def sems(direction, step, piece):
        index = 2 * (step - 1) + piece
        return zs.at[direction, index], zr.at[direction, index]

    def pass_on(direction, step, piece):
        block = slot(direction, step - 1, piece)
        pending.append(send(block, block, *sems(direction, step, piece), ring[direction]))

    def got(direction, step, piece):
        arrived(slot(direction, step, piece), *sems(direction, step, piece), ring[direction])

    half = NZ // 2
    for piece in range(2):
        for direction in range(2):
            pass_on(direction, 1, piece)
    for step in range(2, half + 1):
        for piece in range(2):
            for direction in range(2):
                got(direction, step - 1, piece)
                if step < half or direction == piece:
                    pass_on(direction, step, piece)
    for direction in range(2):
        got(direction, half, direction)
    for copy in pending:
        copy.wait_send()


def norm_and_spread(o, stat, w_out, own_tokens, gain, model_width):
    rows, quarter = own_tokens.shape
    block = (rows, quarter)
    vmem = pl.BlockSpec(memory_space=pltpu.VMEM)
    return pl.pallas_call(
        functools.partial(norm_kernel, model_width),
        out_shape=(
            jax.ShapeDtypeStruct(block, jnp.bfloat16),
            jax.ShapeDtypeStruct((NZ,) + block, jnp.bfloat16),
        ),
        in_specs=[vmem] * 5,
        out_specs=(vmem, vmem),
        scratch_shapes=[
            pltpu.VMEM((NX - 1,) + o.shape[1:], o.dtype),
            pltpu.VMEM((NX - 1,) + stat.shape[1:], stat.dtype),
            pltpu.VMEM((2,) + block, jnp.bfloat16),
            pltpu.VMEM((2,) + block, jnp.bfloat16),
            pltpu.VMEM(block, jnp.bfloat16),
            pltpu.VMEM(block, jnp.bfloat16),
            pltpu.VMEM((rows, 128), jnp.float32),
            pltpu.VMEM((3, rows, 128), jnp.float32),
            pltpu.SemaphoreType.DMA((NX - 1,)),
            pltpu.SemaphoreType.DMA((NX - 1,)),
            pltpu.SemaphoreType.DMA((NX - 1,)),
            pltpu.SemaphoreType.DMA((NX - 1,)),
            pltpu.SemaphoreType.DMA((2,)),
            pltpu.SemaphoreType.DMA((2,)),
            pltpu.SemaphoreType.DMA((1,)),
            pltpu.SemaphoreType.DMA((1,)),
            pltpu.SemaphoreType.DMA((3,)),
            pltpu.SemaphoreType.DMA((3,)),
            pltpu.SemaphoreType.DMA((2, NZ)),
            pltpu.SemaphoreType.DMA((2, NZ)),
        ],
        compiler_params=pltpu.CompilerParams(
            collective_id=2, has_side_effects=True, vmem_limit_bytes=32 * 1024 * 1024
        ),
        name="norm_and_spread",
    )(o, stat, w_out, own_tokens, gain)


def dispatch_kernel(slots, source, rows, sel, held, own_sem, xs, xr, ys, yr, cs, cr):
    rank, tensor = lax.axis_index("expert"), lax.axis_index("tensor")
    y_lo, x, z, y_hi, core, far, sides, mate = corner(rank, tensor)
    other = 1 - y_lo
    x_peers = [(rank_of(y_lo, lax.rem(x + d, NX), z), tensor) for d in range(1, NX)]
    greet(x_peers + [far] + sides + [mate])
    pending = []
    lane = lax.broadcasted_iota(jnp.int32, (slots.shape[2], source.shape[0]), 1)

    def pick(side, to):
        chosen = jnp.where(lane == slots[side, to], 1.0, 0.0).astype(jnp.bfloat16)
        sel[side, to] = jnp.dot(
            chosen, source[...], preferred_element_type=jnp.float32
        ).astype(jnp.bfloat16)

    pick(other, x)
    pick(y_lo, x)
    own = pltpu.make_async_copy(sel.at[y_lo, x], rows.at[tensor, y_lo, x], own_sem.at[0])
    own.start()

    def to_side(d, here, there):
        x_s = lax.rem(x + NX - d, NX)
        spot = rows.at[tensor, y_lo, x_s]
        for r in range(2):
            pending.append(send(there, spot, ys.at[d, r], yr.at[d, r], sides[r]))
        pending.append(send(here, spot, ys.at[d, 2], yr.at[d, 2], far))

    def forward(d, r, l):
        x_s = lax.rem(x + NX - d, NX)
        spot = rows.at[lax.rem(y_hi + r, 2) * 2 + core, lax.rem(y_lo + l, 2), x_s]
        index = 2 * r + l
        pending.append(send(spot, spot, cs.at[d, index], cr.at[d, index], mate))

    to_side(0, sel.at[y_lo, x], sel.at[other, x])
    for d in (2, 1, 3):
        to = lax.rem(x + d, NX)
        for i in range(2):
            pick(other if i == 0 else y_lo, to)
            src = sel.at[other if i == 0 else y_lo, to]
            dst = held.at[x] if i == 0 else rows.at[tensor, y_lo, x]
            pending.append(send(src, dst, xs.at[d - 1, i], xr.at[d - 1, i], x_peers[d - 1]))
    own.wait()
    forward(0, 0, 0)
    for d in (1, 3, 2):
        x_s = lax.rem(x + NX - d, NX)
        arrived(held.at[x_s], xs.at[d - 1, 0], xr.at[d - 1, 0], x_peers[d - 1])
        arrived(rows.at[tensor, y_lo, x_s], xs.at[d - 1, 1], xr.at[d - 1, 1], x_peers[d - 1])
        to_side(d, rows.at[tensor, y_lo, x_s], held.at[x_s])
        forward(d, 0, 0)
    for d in (0, 1, 3, 2):
        x_s = lax.rem(x + NX - d, NX)
        for r in range(2):
            spot = rows.at[lax.rem(y_hi + r, 2) * 2 + core, other, x_s]
            arrived(spot, ys.at[d, r], yr.at[d, r], sides[r])
            forward(d, r, 1)
        spot = rows.at[(1 - y_hi) * 2 + core, y_lo, x_s]
        arrived(spot, ys.at[d, 2], yr.at[d, 2], far)
        forward(d, 1, 0)
    for d in range(NX):
        x_s = lax.rem(x + NX - d, NX)
        for r in range(2):
            for l in range(2):
                spot = rows.at[lax.rem(y_hi + r, 2) * 2 + 1 - core, lax.rem(y_lo + l, 2), x_s]
                arrived(spot, cs.at[d, 2 * r + l], cr.at[d, 2 * r + l], mate)
    for copy in pending:
        copy.wait_send()


def dispatch(slots, source):
    piece = (slots.shape[2], source.shape[1])
    vmem = pl.BlockSpec(memory_space=pltpu.VMEM)
    return pl.pallas_call(
        dispatch_kernel,
        out_shape=jax.ShapeDtypeStruct((4, NY, NX) + piece, source.dtype),
        in_specs=[vmem, vmem],
        out_specs=pl.BlockSpec(memory_space=pl.ANY),
        scratch_shapes=[
            pltpu.VMEM((NY, NX) + piece, source.dtype),
            pltpu.VMEM((NX,) + piece, source.dtype),
            pltpu.SemaphoreType.DMA((1,)),
            pltpu.SemaphoreType.DMA((NX - 1, 2)),
            pltpu.SemaphoreType.DMA((NX - 1, 2)),
            pltpu.SemaphoreType.DMA((NX, 3)),
            pltpu.SemaphoreType.DMA((NX, 3)),
            pltpu.SemaphoreType.DMA((NX, 4)),
            pltpu.SemaphoreType.DMA((NX, 4)),
        ],
        compiler_params=pltpu.CompilerParams(
            collective_id=3, has_side_effects=True, vmem_limit_bytes=32 * 1024 * 1024
        ),
        name="dispatch",
    )(slots, source)


def expert_kernel(rows_ref, up_ref, down_ref, out_ref, up, down):
    quarters, groups, size, width = rows_ref.shape
    count = groups * size
    units, real = down.shape[1], down_ref.shape[0]

    @pl.when(pl.program_id(0) == 0)
    def _():
        blank = jnp.zeros((units - real, width), jnp.bfloat16)
        for q in range(quarters):
            span = slice(q * width, (q + 1) * width)
            for i in range(2):
                up[q, i * units : i * units + real, :] = up_ref[i, :, span]
                up[q, i * units + real : (i + 1) * units, :] = blank
            down[q, :real, :] = down_ref[:, span]
            down[q, real:, :] = blank

    total = jnp.zeros((count, 2 * units), jnp.float32)
    for q in range(quarters):
        total += lax.dot_general(
            rows_ref[q].reshape(count, width), up[q], (((1,), (1,)), ((), ())),
            preferred_element_type=jnp.float32,
        )
    gate, raised = total[:, :units], total[:, units:]
    active = (gate * jax.nn.sigmoid(1.702 * gate) * (raised + 1.0)).astype(jnp.bfloat16)
    for q in range(quarters):
        value = jnp.dot(active, down[q], preferred_element_type=jnp.float32)
        out_ref[q] = value.astype(jnp.bfloat16).reshape(groups, size, width)


def run_expert(rows, up, down):
    quarters, groups, size, width = rows.shape
    step = 2
    units = -(-down.shape[0] // 128) * 128
    block = pl.BlockSpec((quarters, step, size, width), lambda i: (0, i, 0, 0))
    return pl.pallas_call(
        expert_kernel,
        grid=(groups // step,),
        in_specs=[
            block,
            pl.BlockSpec(up.shape, lambda i: (0, 0, 0)),
            pl.BlockSpec(down.shape, lambda i: (0, 0)),
        ],
        out_shape=jax.ShapeDtypeStruct(rows.shape, jnp.bfloat16),
        out_specs=block,
        scratch_shapes=[
            pltpu.VMEM((quarters, 2 * units, width), jnp.bfloat16),
            pltpu.VMEM((quarters, units, width), jnp.bfloat16),
        ],
        compiler_params=pltpu.CompilerParams(vmem_limit_bytes=56 * 1024 * 1024),
        name="run_expert",
    )(rows, up, down)


def collect_kernel(part, out, mine, core_in, side_out, side_in, x_out, ms, cs, cr, ys, yr, xs, xr):
    rank, tensor = lax.axis_index("expert"), lax.axis_index("tensor")
    y_lo, x, z, y_hi, core, far, sides, mate = corner(rank, tensor)
    other = 1 - y_lo
    x_peers = [(rank_of(y_lo, lax.rem(x + d, NX), z), tensor) for d in range(1, NX)]
    greet(x_peers + [far] + sides + [mate])
    pending, loads = [], {}
    order = (2, 1, 3, 0)
    def where(kind):
        half = y_hi if kind in (0, 3) else 1 - y_hi
        return half, (other if kind < 2 else y_lo)

    for d in order:
        x_h = lax.rem(x + d, NX)
        for kind in range(4):
            half, side = where(kind)
            src = part.at[half * 2 + 1 - core, side, x_h]
            pending.append(
                send(src, core_in.at[d, kind], cs.at[d, kind], cr.at[d, kind], mate)
            )
            load = pltpu.make_async_copy(
                part.at[half * 2 + core, side, x_h], mine.at[d, kind], ms.at[d, kind]
            )
            load.start()
            loads[d, kind] = load
    for d in order:
        for kind in range(4):
            arrived(core_in.at[d, kind], cs.at[d, kind], cr.at[d, kind], mate)
            loads[d, kind].wait()
            both = f32(mine[d, kind]) + f32(core_in[d, kind])
            side_out[d, kind] = both.astype(jnp.bfloat16)
            if kind < 3:
                to = far if kind == 2 else sides[kind]
                pending.append(
                    send(
                        side_out.at[d, kind], side_in.at[d, kind], ys.at[d, kind], yr.at[d, kind], to
                    )
                )
    for d in order:
        for kind in range(3):
            to = far if kind == 2 else sides[kind]
            arrived(side_in.at[d, kind], ys.at[d, kind], yr.at[d, kind], to)
            if kind == 0:
                continue
            first = side_in[d, 0] if kind == 1 else side_out[d, 3]
            both = (f32(first) + f32(side_in[d, kind])).astype(jnp.bfloat16)
            i = kind - 1
            owner = other if kind == 1 else y_lo
            if d == 0:
                out[owner, x] = both
            else:
                x_out[d - 1, i] = both
                pending.append(
                    send(
                        x_out.at[d - 1, i], out.at[owner, x], xs.at[d - 1, i], xr.at[d - 1, i],
                        x_peers[d - 1],
                    )
                )
    for d in order[:-1]:
        x_e = lax.rem(x + NX - d, NX)
        for i in range(2):
            owner = other if i == 0 else y_lo
            arrived(out.at[owner, x_e], xs.at[d - 1, i], xr.at[d - 1, i], x_peers[d - 1])
    for copy in pending:
        copy.wait_send()


def collect(part):
    piece = part.shape[3:]
    return pl.pallas_call(
        collect_kernel,
        out_shape=jax.ShapeDtypeStruct(part.shape[1:], part.dtype),
        in_specs=[pl.BlockSpec(memory_space=pl.ANY)],
        out_specs=pl.BlockSpec(memory_space=pltpu.VMEM),
        scratch_shapes=[
            pltpu.VMEM((NX, 4) + piece, jnp.bfloat16),
            pltpu.VMEM((NX, 4) + piece, jnp.bfloat16),
            pltpu.VMEM((NX, 4) + piece, jnp.bfloat16),
            pltpu.VMEM((NX, 3) + piece, jnp.bfloat16),
            pltpu.VMEM((NX - 1, 2) + piece, jnp.bfloat16),
            pltpu.SemaphoreType.DMA((NX, 4)),
            pltpu.SemaphoreType.DMA((NX, 4)),
            pltpu.SemaphoreType.DMA((NX, 4)),
            pltpu.SemaphoreType.DMA((NX, 3)),
            pltpu.SemaphoreType.DMA((NX, 3)),
            pltpu.SemaphoreType.DMA((NX - 1, 2)),
            pltpu.SemaphoreType.DMA((NX - 1, 2)),
        ],
        compiler_params=pltpu.CompilerParams(
            collective_id=4, has_side_effects=True, vmem_limit_bytes=48 * 1024 * 1024
        ),
        name="collect",
    )(part)


def home_kernel(slots, weights, rows_in, hidden, out, sums, staged, landed, zs, zr):
    rank, tensor = lax.axis_index("expert"), lax.axis_index("tensor")
    y_lo, x, z = place_of(rank)
    ring = [
        (rank_of(y_lo, x, lax.rem(z + 1, NZ)), tensor),
        (rank_of(y_lo, x, lax.rem(z + NZ - 1, NZ)), tensor),
    ]
    greet(ring)
    count = hidden.shape[0]
    rows = count // 2
    half = NZ // 2
    pending = []
    row = lax.broadcasted_iota(jnp.int32, (count, slots.shape[1]), 0)

    def add_up(home):
        share = jnp.where(row + home * count == slots[...], weights[...], 0.0)
        sums[home] = jnp.dot(
            share.astype(jnp.bfloat16), rows_in[...], preferred_element_type=jnp.float32
        ).astype(jnp.bfloat16)

    def reach(direction, piece):
        return half if direction == piece else half - 1

    def got(direction, steps, piece):
        index = 2 * steps + piece
        arrived(
            landed.at[direction, index], zs.at[direction, index], zr.at[direction, index],
            ring[direction],
        )
        return f32(landed[direction, index])

    for steps in range(half, 0, -1):
        add_up(lax.rem(z + steps, NZ))
        if steps < half:
            add_up(lax.rem(z + NZ - steps, NZ))
        for piece in range(2):
            for direction in range(2):
                if steps > reach(direction, piece):
                    continue
                home = lax.rem(z + (steps if direction == 0 else NZ - steps), NZ)
                mine = f32(sums[home, pl.ds(piece * rows, rows)])
                if steps < reach(direction, piece):
                    mine = mine + got(direction, steps, piece)
                index = 2 * (steps - 1) + piece
                staged[direction, index] = mine.astype(jnp.bfloat16)
                pending.append(
                    send(
                        staged.at[direction, index], landed.at[direction, index],
                        zs.at[direction, index], zr.at[direction, index], ring[direction],
                    )
                )
    add_up(z)
    for piece in range(2):
        span = pl.ds(piece * rows, rows)
        total = f32(sums[z, span])
        for direction in range(2):
            total = total + got(direction, 0, piece)
        out[span] = (f32(hidden[span]) + total).astype(jnp.bfloat16)
    for copy in pending:
        copy.wait_send()


def bring_home(slots, weights, rows_in, hidden):
    rows, width = hidden.shape
    vmem = pl.BlockSpec(memory_space=pltpu.VMEM)
    return pl.pallas_call(
        home_kernel,
        out_shape=jax.ShapeDtypeStruct(hidden.shape, hidden.dtype),
        in_specs=[vmem] * 4,
        out_specs=vmem,
        scratch_shapes=[
            pltpu.VMEM((NZ, rows, width), jnp.bfloat16),
            pltpu.VMEM((2, NZ, rows // 2, width), jnp.bfloat16),
            pltpu.VMEM((2, NZ, rows // 2, width), jnp.bfloat16),
            pltpu.SemaphoreType.DMA((2, NZ)),
            pltpu.SemaphoreType.DMA((2, NZ)),
        ],
        compiler_params=pltpu.CompilerParams(
            collective_id=5, has_side_effects=True, vmem_limit_bytes=32 * 1024 * 1024
        ),
        name="bring_home",
    )(slots, weights, rows_in, hidden)


def route_kernel(capacity, routed, weights, slab):
    experts, _ = slab.shape
    top_count, count = routed.shape
    row = lax.broadcasted_iota(jnp.int32, (experts, count), 0)
    lane = lax.broadcasted_iota(jnp.int32, (experts, count), 1)
    expert = lax.rem(row, experts // NZ) * NZ + row // (experts // NZ)
    before = jnp.where(
        lax.broadcasted_iota(jnp.int32, (count, count), 0)
        < lax.broadcasted_iota(jnp.int32, (count, count), 1),
        1.0,
        0.0,
    ).astype(jnp.bfloat16)
    token = f32(lane + 1)
    earlier = jnp.zeros((experts, 1), jnp.float32)
    arrivals, shares = [], []
    for k in range(top_count):
        hit = jnp.where(expert == routed[k : k + 1, :], 1.0, 0.0)
        ahead = jnp.dot(hit.astype(jnp.bfloat16), before, preferred_element_type=jnp.float32)
        arrivals.append(jnp.where(hit > 0.0, ahead + earlier, -1.0))
        shares.append(weights[k : k + 1, :])
        earlier = earlier + jnp.sum(hit, axis=1, keepdims=True)
    tokens, scales = jnp.full((experts, 128), -1.0, jnp.float32), jnp.zeros(
        (experts, 128), jnp.float32
    )
    slot = lax.broadcasted_iota(jnp.int32, (experts, 128), 1)
    for place in range(capacity):
        named = jnp.zeros((experts, count), jnp.float32)
        scale = jnp.zeros((experts, count), jnp.float32)
        for k in range(top_count):
            here = arrivals[k] == float(place)
            named = jnp.where(here, token, named)
            scale = jnp.where(here, shares[k], scale)
        tokens = jnp.where(slot == place, jnp.sum(named, axis=1, keepdims=True) - 1.0, tokens)
        scales = jnp.where(slot == place, jnp.sum(scale, axis=1, keepdims=True), scales)
    slab[:, :128] = tokens
    slab[:, 128:] = scales


def routing_slab(routed, weights, expert_count, capacity):
    vmem = pl.BlockSpec(memory_space=pltpu.VMEM)
    slab = pl.pallas_call(
        functools.partial(route_kernel, capacity),
        out_shape=jax.ShapeDtypeStruct((expert_count, 256), jnp.float32),
        in_specs=[vmem, vmem],
        out_specs=vmem,
        name="route",
    )(routed, weights)
    return slab.reshape(NZ, expert_count // NZ, 256)


def on_device(
    tokens,
    attn_gain,
    w_query,
    key_value_weight,
    w_out,
    cache_keyval,
    prefix_length,
    routed_experts,
    route_weights,
    expert_gain,
    w_gate_up,
    w_down,
):
    span_dev, seq_count, quarter = tokens.shape
    model_width = attn_gain.shape[0]
    row_count = span_dev * seq_count
    head_dim = key_value_weight.shape[2] // 2
    cache_rows = cache_keyval.shape[0]
    tensor_rank = lax.axis_index("tensor")
    expert_rank = lax.axis_index("expert")
    quarters = model_width // quarter
    top_count = routed_experts.shape[2]
    expert_count = lax.axis_size("expert")
    capacity = min(row_count, max(2, 5 * row_count * top_count // (2 * expert_count)))
    half_dim = head_dim // 2
    steps_up = jnp.arange(half_dim, dtype=jnp.float32)
    frequency = jnp.exp(steps_up * (-math.log(ROPE_BASE) / half_dim))
    span_place = expert_rank * span_dev + jnp.arange(span_dev, dtype=jnp.int32)
    places = (prefix_length[:, None] + span_place[None, :]).reshape(row_count).astype(jnp.float32)
    angles = frequency[:, None] * places[None, :]
    slab = routing_slab(
        routed_experts.transpose(2, 1, 0).reshape(top_count, row_count),
        route_weights.transpose(2, 1, 0).reshape(top_count, row_count),
        expert_count,
        capacity,
    )
    own_tokens = tokens.transpose(1, 0, 2).reshape(row_count, quarter)
    fresh, kv_all, q_all, slab_all = front(
        head_dim ** (-0.5) * LOG2E,
        own_tokens,
        attn_gain.reshape(quarters, 1, quarter),
        w_query,
        key_value_weight[:, 0, :],
        jnp.cos(angles),
        jnp.sin(angles),
        cache_keyval[:, :, 0, :].transpose(1, 0, 2),
        slab,
    )
    new_key_value_rows = fresh.transpose(1, 0, 2)[:, :, None, :]
    place = jnp.concatenate([prefix_length, expert_rank.astype(jnp.int32).reshape(1)])
    part, stat = attend(place, q_all, kv_all, cache_rows)
    gain = lax.dynamic_slice_in_dim(expert_gain, tensor_rank * quarter, quarter, 0)
    hidden, spread = norm_and_spread(
        part, stat, w_out.T, own_tokens, gain.reshape(1, quarter), model_width
    )
    token = slab_all[:, :, :capacity].astype(jnp.int32)
    first = jnp.arange(NZ, dtype=jnp.int32)[:, None, None] * row_count
    slot_token = jnp.where(token >= 0, token + first, -1).transpose(1, 0, 2)
    slot_weight = slab_all[:, :, 128 : 128 + capacity].transpose(1, 0, 2)
    groups, size = NY * NX, NZ * capacity
    rows = dispatch(
        slot_token.reshape(NY, NX, size, 1), spread.reshape(NZ * row_count, quarter)
    )
    value = run_expert(
        rows.reshape(quarters, groups, size, quarter),
        w_gate_up[0].transpose(1, 2, 0),
        w_down[0],
    )
    returned = collect(value.reshape(quarters, NY, NX, size, quarter))
    layer_output = bring_home(
        slot_token.reshape(1, groups * size),
        slot_weight.reshape(1, groups * size),
        returned.reshape(groups * size, quarter),
        hidden,
    )
    layer_output = layer_output.reshape(seq_count, span_dev, quarter).transpose(1, 0, 2)
    return (layer_output, new_key_value_rows)


def solution(mesh):
    return jax.shard_map(
        on_device,
        mesh=mesh,
        in_specs=(
            P("expert", None, "tensor"),
            P(),
            P(None, "tensor"),
            P(None, "tensor", None),
            P("tensor", None),
            P("expert", None, "tensor", None),
            P(),
            P("expert", None, None),
            P("expert", None, None),
            P(),
            P("expert", None, None, "tensor"),
            P("expert", "tensor", None),
        ),
        out_specs=(P("expert", None, "tensor"), P("expert", None, "tensor", None)),
        check_vma=False,
    )
```

time: 409 us -> 299 us (0.73)
  local copies, waits for them, and re-layouts: 87.1 us -> 17.7 us
  other arithmetic: 18.3 us -> 1.69 us
  blocking collectives: 13.9 us -> 0 us
  matrix products: 6.46 us -> 0 us
    reshape x10 -> x5, local copies, waits for them, and re-layouts: 30.5 us -> 4.06 us  [the longest x1 1.07 us: on_device(): slot_token.reshape(NY, NX, size, 1)]
    pallas_call x6 -> x4, Pallas kernels: 151 us -> 136 us  [the longest x1 61.5 us: dispatch(): pl.pallas_call(dispatch_kernel, out_shape=jax.ShapeDtypeStruct((4, NY, NX...]
    all_gather x1 -> x0, blocking collectives: 13.9 us -> none  [on_device(): shard_piece = lax.all_gather(tokens, 'tensor', axis=2, tiled=True)]
    convert_element_type x7 -> x1, local copies, waits for them, and re-layouts: 13.6 us -> 0.08 us  [on_device(): (prefix_length[:, None] + span_place[None, :]).reshape(row_count)]
    pallas_call x1, Pallas kernels: 35.8 us -> 47.6 us  [norm_and_spread(): pl.pallas_call(functools.partial(norm_kernel, model_width), out_shape=(ja...]
    unnamed x70 -> x18, local copies, waits for them, and re-layouts: 20.6 us -> 10.2 us
    pad x2 -> x0, local copies, waits for them, and re-layouts: 7.84 us -> none  [the longest x1 4.61 us: on_device(): up = jnp.pad(w_gate_up[0], ((0, 0), (0, 0), (0, units - ffn_local)))]
    dot_general x3 -> x0, matrix products: 6.46 us -> none  [the longest x1 2.87 us: on_device(): query_acc = jnp.dot(rescaled, w_query, preferred_element_type=jnp.float32)]
where the time goes in v3:
time: 299 us; the launch traced here: 298 us
  Pallas kernels  278 us (93%)
  local copies, waits for them, and re-layouts  17.7 us (6%)
    pallas_call x1, Pallas kernels, dispatch(): pl.pallas_call(dispatch_kernel, out_shape=jax.ShapeDtypeStruct((4, NY, NX...  61.5 us
    pallas_call x1, Pallas kernels, collect(): pl.pallas_call(collect_kernel, out_shape=jax.ShapeDtypeStruct(part.shape[...  49.3 us
    pallas_call x1, Pallas kernels, norm_and_spread(): pl.pallas_call(functools.partial(norm_kernel, model_width), out_shape=(ja...  47.6 us
    pallas_call x1, Pallas kernels, front(): pl.pallas_call(functools.partial(front_kernel, scale), out_shape=(jax.Sha...  38.3 us
    pallas_call x1, Pallas kernels, attend(): pl.pallas_call(functools.partial(attend_kernel, cache_rows), grid=(seqs,...  34.1 us
    pallas_call x1, Pallas kernels, bring_home(): pl.pallas_call(home_kernel, out_shape=jax.ShapeDtypeStruct(hidden.shape,...  23.3 us
    pallas_call x1, Pallas kernels, run_expert(): pl.pallas_call(expert_kernel, grid=(groups // step,), in_specs=[block, pl...  21.8 us
    unnamed x18, local copies, waits for them, and re-layouts  10.2 us

profile of v3, /device:TPU:40, one launch (start us, length us, event | category | flops | bytes accessed | tf_op | source)
XLA Modules:
  0.0 298.0 jit_solution(2554951051042889708)
XLA Ops:
  0.6 0.7 pad_add_fusion.place
  1.4 0.7 add_convert_fusion
  2.2 0.8 dynamic_slice.3
  3.0 0.7 copy.25
  4.3 0.7 copy.26
  5.7 0.8 reshape.80.gain
  6.6 1.9 route.1
  8.5 0.9 copy.36
  9.4 1.0 copy.23
  10.4 1.8 copy-done.1
  12.2 1.1 copy-done.4
  13.3 0.8 copy-done.7
  14.2 38.3 %front.1 = (bf16[2,64,128]{2,1,0:T(8,128)(2,1)S(1)}, bf16[16,2,256,128]{3,2,1,0:T(8,128)(2,1)S(1)}, bf16[4,2,64,512]{3,2,1,0:T(8,128)(2,1)S(1)}, f32[8,8,256]{2,1,0:T(8,128)S(1)}) custom-call(bf16[128,720]{1,0:T(8,128)(2,1)S(1)} %bitcast.35, f32[4,1,720]{2,1,0:T(1,128)S(1)} %reshape.80.gain, bf16[2880,512]{1,0:T(8,128)(2,1)S(1)} %copy-done.1, ...), custom_call_target="tpu_custom_call" | custom-call | tf_op jit(solution)/shard_map/front/pallas_call | solution.py:220
  52.5 34.1 %attend.1 = (bf16[4,2,64,512]{3,2,1,0:T(8,128)(2,1)S(1)}, f32[4,2,8,512]{3,2,1,0:T(8,128)S(1)}) custom-call(s32[3]{0:T(128)S(1)} %pad_add_fusion.place, bf16[4,2,64,512]{3,2,1,0:T(8,128)(2,1)S(1)} %get-tuple-element.11.q_ref, bf16[16,2,256,128]{3,2,1,0:T(8,128)(2,1)S(1)} %get-tuple-element.12.kv_ref), custom_call_target="tpu_custom_call" | custom-call | tf_op jit(solution)/shard_map/attend/pallas_call | solution.py:325
  86.6 0.8 copy-done.5
  88.4 1.1 reshape.94.slots
  89.5 1.0 copy-done.6
  90.5 47.6 %norm_and_spread.1 = (bf16[128,720]{1,0:T(8,128)(2,1)S(1)}, bf16[8,128,720]{2,1,0:T(8,128)(2,1)S(1)}) custom-call(bf16[4,2,64,512]{3,2,1,0:T(8,128)(2,1)S(1)} %copy-done.6, f32[4,2,8,512]{3,2,1,0:T(8,128)S(1)} %get-tuple-element.14.stat, bf16[2880,512]{1,0:T(8,128)(2,1)S(1)} %bitcast.34, bf16[128,720]{1,0:T(8,128)(2,1)S(1)} %bitcast.36, ...), custom_call_target="tpu_custom_call" | custom-call | tf_op jit(solution)/shard_map/norm_and_spread/pallas_call | solution.py:480
  138.1 61.5 %dispatch.1 = bf16[4,2,4,160,720]{4,3,2,1,0:T(8,128)(2,1)S(1)} custom-call(s32[2,4,160,1]{3,2,1,0:T(8,128)S(1)} %copy-done.3, bf16[1024,720]{1,0:T(8,128)(2,1)S(1)} %bitcast.37), custom_call_target="tpu_custom_call" | custom-call | tf_op jit(solution)/shard_map/dispatch/pallas_call | solution.py:588
  199.6 3.0 %copy-done = bf16[4,2,4,160,720]{4,3,2,1,0:T(8,128)(2,1)} copy-done((bf16[4,2,4,160,720]{4,3,2,1,0:T(8,128)(2,1)}, bf16[4,2,4,160,720]{4,3,2,1,0:T(8,128)(2,1)S(1)}, u32[]{:S(2)}) %copy-start) | copy-done | bytes 7372824
  202.7 21.8 %run_expert.1 = bf16[4,8,160,720]{3,2,1,0:T(8,128)(2,1)} custom-call(bf16[4,8,160,720]{3,2,1,0:T(8,128)(2,1)} %bitcast.32, bf16[2,360,2880]{2,1,0:T(8,128)(2,1)} %bitcast.44, bf16[360,2880]{1,0:T(8,128)(2,1)} %bitcast.45), custom_call_target="tpu_custom_call" | custom-call | tf_op jit(solution)/shard_map/run_expert/pallas_call | solution.py:645
  224.5 49.3 %collect.1 = bf16[2,4,160,720]{3,2,1,0:T(8,128)(2,1)S(1)} custom-call(bf16[4,2,4,160,720]{4,3,2,1,0:T(8,128)(2,1)} %bitcast.43), custom_call_target="tpu_custom_call" | custom-call | tf_op jit(solution)/shard_map/collect/pallas_call | solution.py:733
  273.8 23.3 %bring_home.1 = bf16[128,720]{1,0:T(8,128)(2,1)S(1)} custom-call(s32[1,1280]{1,0:T(1,128)S(1)} %reshape.84.slots, f32[1,1280]{1,0:T(1,128)S(1)} %reshape.85.weights, bf16[1280,720]{1,0:T(8,128)(2,1)S(1)} %bitcast.33, bf16[128,720]{1,0:T(8,128)(2,1)S(1)} %get-tuple-element.16.hidden), custom_call_target="tpu_custom_call" | custom-call | tf_op jit(solution)/shard_map/bring_home/pallas_call | solution.py:824
  297.1 0.9 copy.35
  (25 shorter events, 2.5 us)
Async XLA Ops:
  10.4 1.8 copy-start.1
  12.2 1.1 copy-start.4
  13.3 0.8 copy-start.7
  14.2 75.3 %copy-start.2 = (bf16[512,2880]{0,1:T(8,128)(2,1)S(1)}, bf16[512,2880]{0,1:T(8,128)(2,1)}, u32[]{:S(2)}) copy-start(bf16[512,2880]{0,1:T(8,128)(2,1)} %param.16) | copy-start | bytes 8847364
  86.6 0.8 copy-start.5
  89.5 1.0 copy-start.6
  90.5 47.6 %copy-start.3 = (s32[2,4,160,1]{3,2,1,0:T(8,128)S(1)}, s32[2,4,160,1]{3,2,1,0:T(8,128)}, u32[]{:S(2)}) copy-start(s32[2,4,160,1]{3,2,1,0:T(8,128)} %reshape.94.slots) | copy-start | bytes 15364
  199.6 3.1 %copy-start = (bf16[4,2,4,160,720]{4,3,2,1,0:T(8,128)(2,1)}, bf16[4,2,4,160,720]{4,3,2,1,0:T(8,128)(2,1)S(1)}, u32[]{:S(2)}) copy-start(bf16[4,2,4,160,720]{4,3,2,1,0:T(8,128)(2,1)S(1)} %dispatch.1) | copy-start | bytes 22118404

commit v4 on v3

--- a/solution.py
+++ b/solution.py
@@ -514,29 +514,35 @@
     )(o, stat, w_out, own_tokens, gain)
 
 
-def dispatch_kernel(slots, source, rows, sel, held, own_sem, xs, xr, ys, yr, cs, cr):
+def expert_kernel(
+    slots, source, up_hbm, down_hbm, out,
+    rows, sel, held, up_raw, down_raw, up, down, mine, to_mate, core_in, side_in, x_out,
+    ws, xs, xr, ys, yr, fs, fr, cs, cr, bs, br, es, er,
+):
     rank, tensor = lax.axis_index("expert"), lax.axis_index("tensor")
     y_lo, x, z, y_hi, core, far, sides, mate = corner(rank, tensor)
     other = 1 - y_lo
     x_peers = [(rank_of(y_lo, lax.rem(x + d, NX), z), tensor) for d in range(1, NX)]
     greet(x_peers + [far] + sides + [mate])
     pending = []
-    lane = lax.broadcasted_iota(jnp.int32, (slots.shape[2], source.shape[0]), 1)
+    loads = [
+        pltpu.make_async_copy(up_hbm, up_raw, ws.at[0]),
+        pltpu.make_async_copy(down_hbm, down_raw, ws.at[1]),
+    ]
+    for load in loads:
+        load.start()
+    size, width = sel.shape[2:]
+    quarters = rows.shape[0]
+    lane = lax.broadcasted_iota(jnp.int32, (size, source.shape[0]), 1)
 
     def pick(side, to):
         chosen = jnp.where(lane == slots[side, to], 1.0, 0.0).astype(jnp.bfloat16)
-        sel[side, to] = jnp.dot(
-            chosen, source[...], preferred_element_type=jnp.float32
-        ).astype(jnp.bfloat16)
-
-    pick(other, x)
-    pick(y_lo, x)
-    own = pltpu.make_async_copy(sel.at[y_lo, x], rows.at[tensor, y_lo, x], own_sem.at[0])
-    own.start()
+        return jnp.dot(chosen, source[...], preferred_element_type=jnp.float32).astype(
+            jnp.bfloat16
+        )
 
     def to_side(d, here, there):
-        x_s = lax.rem(x + NX - d, NX)
-        spot = rows.at[tensor, y_lo, x_s]
+        spot = rows.at[tensor, y_lo, lax.rem(x + NX - d, NX)]
         for r in range(2):
             pending.append(send(there, spot, ys.at[d, r], yr.at[d, r], sides[r]))
         pending.append(send(here, spot, ys.at[d, 2], yr.at[d, 2], far))
@@ -545,25 +551,9 @@
         x_s = lax.rem(x + NX - d, NX)
         spot = rows.at[lax.rem(y_hi + r, 2) * 2 + core, lax.rem(y_lo + l, 2), x_s]
         index = 2 * r + l
-        pending.append(send(spot, spot, cs.at[d, index], cr.at[d, index], mate))
-
-    to_side(0, sel.at[y_lo, x], sel.at[other, x])
-    for d in (2, 1, 3):
-        to = lax.rem(x + d, NX)
-        for i in range(2):
-            pick(other if i == 0 else y_lo, to)
-            src = sel.at[other if i == 0 else y_lo, to]
-            dst = held.at[x] if i == 0 else rows.at[tensor, y_lo, x]
-            pending.append(send(src, dst, xs.at[d - 1, i], xr.at[d - 1, i], x_peers[d - 1]))
-    own.wait()
-    forward(0, 0, 0)
-    for d in (1, 3, 2):
-        x_s = lax.rem(x + NX - d, NX)
-        arrived(held.at[x_s], xs.at[d - 1, 0], xr.at[d - 1, 0], x_peers[d - 1])
-        arrived(rows.at[tensor, y_lo, x_s], xs.at[d - 1, 1], xr.at[d - 1, 1], x_peers[d - 1])
-        to_side(d, rows.at[tensor, y_lo, x_s], held.at[x_s])
-        forward(d, 0, 0)
-    for d in (0, 1, 3, 2):
+        pending.append(send(spot, spot, fs.at[d, index], fr.at[d, index], mate))
+
+    def from_sides(d):
         x_s = lax.rem(x + NX - d, NX)
         for r in range(2):
             spot = rows.at[lax.rem(y_hi + r, 2) * 2 + core, other, x_s]
@@ -572,188 +562,175 @@
         spot = rows.at[(1 - y_hi) * 2 + core, y_lo, x_s]
         arrived(spot, ys.at[d, 2], yr.at[d, 2], far)
         forward(d, 1, 0)
-    for d in range(NX):
+
+    def from_mate(d):
         x_s = lax.rem(x + NX - d, NX)
         for r in range(2):
             for l in range(2):
                 spot = rows.at[lax.rem(y_hi + r, 2) * 2 + 1 - core, lax.rem(y_lo + l, 2), x_s]
-                arrived(spot, cs.at[d, 2 * r + l], cr.at[d, 2 * r + l], mate)
-    for copy in pending:
-        copy.wait_send()
-
-
-def dispatch(slots, source):
-    piece = (slots.shape[2], source.shape[1])
-    vmem = pl.BlockSpec(memory_space=pltpu.VMEM)
-    return pl.pallas_call(
-        dispatch_kernel,
-        out_shape=jax.ShapeDtypeStruct((4, NY, NX) + piece, source.dtype),
-        in_specs=[vmem, vmem],
-        out_specs=pl.BlockSpec(memory_space=pl.ANY),
-        scratch_shapes=[
-            pltpu.VMEM((NY, NX) + piece, source.dtype),
-            pltpu.VMEM((NX,) + piece, source.dtype),
-            pltpu.SemaphoreType.DMA((1,)),
-            pltpu.SemaphoreType.DMA((NX - 1, 2)),
-            pltpu.SemaphoreType.DMA((NX - 1, 2)),
-            pltpu.SemaphoreType.DMA((NX, 3)),
-            pltpu.SemaphoreType.DMA((NX, 3)),
-            pltpu.SemaphoreType.DMA((NX, 4)),
-            pltpu.SemaphoreType.DMA((NX, 4)),
-        ],
-        compiler_params=pltpu.CompilerParams(
-            collective_id=3, has_side_effects=True, vmem_limit_bytes=32 * 1024 * 1024
-        ),
-        name="dispatch",
-    )(slots, source)
-
-
-def expert_kernel(rows_ref, up_ref, down_ref, out_ref, up, down):
-    quarters, groups, size, width = rows_ref.shape
-    count = groups * size
-    units, real = down.shape[1], down_ref.shape[0]
-
-    @pl.when(pl.program_id(0) == 0)
-    def _():
-        blank = jnp.zeros((units - real, width), jnp.bfloat16)
+                arrived(spot, fs.at[d, 2 * r + l], fr.at[d, 2 * r + l], mate)
+
+    units, real = down.shape[1], down_raw.shape[0]
+
+    def run(d):
+        x_s = lax.rem(x + NX - d, NX)
+        total = jnp.zeros((2 * size, 2 * units), jnp.float32)
         for q in range(quarters):
-            span = slice(q * width, (q + 1) * width)
-            for i in range(2):
-                up[q, i * units : i * units + real, :] = up_ref[i, :, span]
-                up[q, i * units + real : (i + 1) * units, :] = blank
-            down[q, :real, :] = down_ref[:, span]
-            down[q, real:, :] = blank
-
-    total = jnp.zeros((count, 2 * units), jnp.float32)
-    for q in range(quarters):
-        total += lax.dot_general(
-            rows_ref[q].reshape(count, width), up[q], (((1,), (1,)), ((), ())),
-            preferred_element_type=jnp.float32,
-        )
-    gate, raised = total[:, :units], total[:, units:]
-    active = (gate * jax.nn.sigmoid(1.702 * gate) * (raised + 1.0)).astype(jnp.bfloat16)
-    for q in range(quarters):
-        value = jnp.dot(active, down[q], preferred_element_type=jnp.float32)
-        out_ref[q] = value.astype(jnp.bfloat16).reshape(groups, size, width)
-
-
-def run_expert(rows, up, down):
-    quarters, groups, size, width = rows.shape
-    step = 2
-    units = -(-down.shape[0] // 128) * 128
-    block = pl.BlockSpec((quarters, step, size, width), lambda i: (0, i, 0, 0))
-    return pl.pallas_call(
-        expert_kernel,
-        grid=(groups // step,),
-        in_specs=[
-            block,
-            pl.BlockSpec(up.shape, lambda i: (0, 0, 0)),
-            pl.BlockSpec(down.shape, lambda i: (0, 0)),
-        ],
-        out_shape=jax.ShapeDtypeStruct(rows.shape, jnp.bfloat16),
-        out_specs=block,
-        scratch_shapes=[
-            pltpu.VMEM((quarters, 2 * units, width), jnp.bfloat16),
-            pltpu.VMEM((quarters, units, width), jnp.bfloat16),
-        ],
-        compiler_params=pltpu.CompilerParams(vmem_limit_bytes=56 * 1024 * 1024),
-        name="run_expert",
-    )(rows, up, down)
-
-
-def collect_kernel(part, out, mine, core_in, side_out, side_in, x_out, ms, cs, cr, ys, yr, xs, xr):
-    rank, tensor = lax.axis_index("expert"), lax.axis_index("tensor")
-    y_lo, x, z, y_hi, core, far, sides, mate = corner(rank, tensor)
-    other = 1 - y_lo
-    x_peers = [(rank_of(y_lo, lax.rem(x + d, NX), z), tensor) for d in range(1, NX)]
-    greet(x_peers + [far] + sides + [mate])
-    pending, loads = [], {}
-    order = (2, 1, 3, 0)
-    def where(kind):
-        half = y_hi if kind in (0, 3) else 1 - y_hi
-        return half, (other if kind < 2 else y_lo)
-
-    for d in order:
-        x_h = lax.rem(x + d, NX)
-        for kind in range(4):
-            half, side = where(kind)
-            src = part.at[half * 2 + 1 - core, side, x_h]
-            pending.append(
-                send(src, core_in.at[d, kind], cs.at[d, kind], cr.at[d, kind], mate)
+            block = jnp.concatenate([rows[q, other, x_s], rows[q, y_lo, x_s]], axis=0)
+            total += lax.dot_general(
+                block, up[q], (((1,), (1,)), ((), ())), preferred_element_type=jnp.float32
             )
-            load = pltpu.make_async_copy(
-                part.at[half * 2 + core, side, x_h], mine.at[d, kind], ms.at[d, kind]
-            )
-            load.start()
-            loads[d, kind] = load
-    for d in order:
+        gate, raised = total[:, :units], total[:, units:]
+        active = (gate * jax.nn.sigmoid(1.702 * gate) * (raised + 1.0)).astype(jnp.bfloat16)
+        for h in range(2):
+            half = lax.rem(y_hi + h, 2)
+            for owner in range(2):
+                index = half * 2 + (core if owner else 1 - core)
+                value = jnp.dot(active, down[index], preferred_element_type=jnp.float32).astype(
+                    jnp.bfloat16
+                )
+                into = mine if owner else to_mate
+                into[d, h] = value[:size]
+                into[d, 3 - h] = value[size:]
+                if not owner:
+                    for kind in (h, 3 - h):
+                        pending.append(
+                            send(
+                                to_mate.at[d, kind], core_in.at[d, kind],
+                                cs.at[d, kind], cr.at[d, kind], mate,
+                            )
+                        )
+
+    def back_to_sides(d):
         for kind in range(4):
             arrived(core_in.at[d, kind], cs.at[d, kind], cr.at[d, kind], mate)
-            loads[d, kind].wait()
             both = f32(mine[d, kind]) + f32(core_in[d, kind])
-            side_out[d, kind] = both.astype(jnp.bfloat16)
+            mine[d, kind] = both.astype(jnp.bfloat16)
             if kind < 3:
                 to = far if kind == 2 else sides[kind]
                 pending.append(
-                    send(
-                        side_out.at[d, kind], side_in.at[d, kind], ys.at[d, kind], yr.at[d, kind], to
-                    )
+                    send(mine.at[d, kind], side_in.at[d, kind], bs.at[d, kind], br.at[d, kind], to)
                 )
-    for d in order:
+
+    def back_to_x(d):
         for kind in range(3):
             to = far if kind == 2 else sides[kind]
-            arrived(side_in.at[d, kind], ys.at[d, kind], yr.at[d, kind], to)
+            arrived(side_in.at[d, kind], bs.at[d, kind], br.at[d, kind], to)
             if kind == 0:
                 continue
-            first = side_in[d, 0] if kind == 1 else side_out[d, 3]
+            first = side_in[d, 0] if kind == 1 else mine[d, 3]
             both = (f32(first) + f32(side_in[d, kind])).astype(jnp.bfloat16)
             i = kind - 1
             owner = other if kind == 1 else y_lo
             if d == 0:
                 out[owner, x] = both
             else:
+                e = NX - d - 1
                 x_out[d - 1, i] = both
                 pending.append(
-                    send(
-                        x_out.at[d - 1, i], out.at[owner, x], xs.at[d - 1, i], xr.at[d - 1, i],
-                        x_peers[d - 1],
-                    )
+                    send(x_out.at[d - 1, i], out.at[owner, x], es.at[e, i], er.at[e, i], x_peers[e])
                 )
-    for d in order[:-1]:
+
+    sel[other, x] = pick(other, x)
+    rows[tensor, y_lo, x] = pick(y_lo, x)
+    to_side(0, rows.at[tensor, y_lo, x], sel.at[other, x])
+    for d in (1, 3, 2):
+        to = lax.rem(x + d, NX)
+        for i in range(2):
+            side = other if i == 0 else y_lo
+            sel[side, to] = pick(side, to)
+            dst = held.at[x] if i == 0 else rows.at[tensor, y_lo, x]
+            pending.append(
+                send(sel.at[side, to], dst, xs.at[d - 1, i], xr.at[d - 1, i], x_peers[d - 1])
+            )
+    forward(0, 0, 0)
+    blank = jnp.zeros((units - real, width), jnp.bfloat16)
+    for load in loads:
+        load.wait()
+    for q in range(quarters):
+        span = slice(q * width, (q + 1) * width)
+        for i in range(2):
+            up[q, i * units : i * units + real, :] = up_raw[i, :, span]
+            up[q, i * units + real : (i + 1) * units, :] = blank
+        down[q, :real, :] = down_raw[:, span]
+        down[q, real:, :] = blank
+
+    def from_x(d):
+        x_s = lax.rem(x + NX - d, NX)
+        arrived(held.at[x_s], xs.at[d - 1, 0], xr.at[d - 1, 0], x_peers[d - 1])
+        arrived(rows.at[tensor, y_lo, x_s], xs.at[d - 1, 1], xr.at[d - 1, 1], x_peers[d - 1])
+        to_side(d, rows.at[tensor, y_lo, x_s], held.at[x_s])
+        forward(d, 0, 0)
+
+    from_x(1)
+    from_x(3)
+    from_sides(0)
+    from_x(2)
+    for d in (0, 1, 3, 2):
+        if d:
+            from_sides(d)
+        from_mate(d)
+        run(d)
+        if d in (1, 3):
+            back_to_sides(d)
+    back_to_sides(2)
+    back_to_sides(0)
+    for d in (1, 3, 2, 0):
+        back_to_x(d)
+    for d in range(1, NX):
         x_e = lax.rem(x + NX - d, NX)
         for i in range(2):
             owner = other if i == 0 else y_lo
-            arrived(out.at[owner, x_e], xs.at[d - 1, i], xr.at[d - 1, i], x_peers[d - 1])
+            arrived(out.at[owner, x_e], es.at[d - 1, i], er.at[d - 1, i], x_peers[d - 1])
     for copy in pending:
         copy.wait_send()
 
 
-def collect(part):
-    piece = part.shape[3:]
+def run_experts(slots, source, up, down):
+    width = source.shape[1]
+    piece = (slots.shape[2], width)
+    quarters = down.shape[1] // width
+    units = -(-down.shape[0] // 128) * 128
+    vmem = pl.BlockSpec(memory_space=pltpu.VMEM)
+    any_space = pl.BlockSpec(memory_space=pl.ANY)
+    bf16, sem = jnp.bfloat16, pltpu.SemaphoreType.DMA
     return pl.pallas_call(
-        collect_kernel,
-        out_shape=jax.ShapeDtypeStruct(part.shape[1:], part.dtype),
-        in_specs=[pl.BlockSpec(memory_space=pl.ANY)],
-        out_specs=pl.BlockSpec(memory_space=pltpu.VMEM),
+        expert_kernel,
+        out_shape=jax.ShapeDtypeStruct((NY, NX) + piece, bf16),
+        in_specs=[vmem, vmem, any_space, any_space],
+        out_specs=vmem,
         scratch_shapes=[
-            pltpu.VMEM((NX, 4) + piece, jnp.bfloat16),
-            pltpu.VMEM((NX, 4) + piece, jnp.bfloat16),
-            pltpu.VMEM((NX, 4) + piece, jnp.bfloat16),
-            pltpu.VMEM((NX, 3) + piece, jnp.bfloat16),
-            pltpu.VMEM((NX - 1, 2) + piece, jnp.bfloat16),
-            pltpu.SemaphoreType.DMA((NX, 4)),
-            pltpu.SemaphoreType.DMA((NX, 4)),
-            pltpu.SemaphoreType.DMA((NX, 4)),
-            pltpu.SemaphoreType.DMA((NX, 3)),
-            pltpu.SemaphoreType.DMA((NX, 3)),
-            pltpu.SemaphoreType.DMA((NX - 1, 2)),
-            pltpu.SemaphoreType.DMA((NX - 1, 2)),
+            pltpu.VMEM((quarters, NY, NX) + piece, bf16),
+            pltpu.VMEM((NY, NX) + piece, bf16),
+            pltpu.VMEM((NX,) + piece, bf16),
+            pltpu.VMEM(up.shape, bf16),
+            pltpu.VMEM(down.shape, bf16),
+            pltpu.VMEM((quarters, 2 * units, width), bf16),
+            pltpu.VMEM((quarters, units, width), bf16),
+            pltpu.VMEM((NX, 4) + piece, bf16),
+            pltpu.VMEM((NX, 4) + piece, bf16),
+            pltpu.VMEM((NX, 4) + piece, bf16),
+            pltpu.VMEM((NX, 3) + piece, bf16),
+            pltpu.VMEM((NX - 1, 2) + piece, bf16),
+            sem((2,)),
+            sem((NX - 1, 2)),
+            sem((NX - 1, 2)),
+            sem((NX, 3)),
+            sem((NX, 3)),
+            sem((NX, 4)),
+            sem((NX, 4)),
+            sem((NX, 4)),
+            sem((NX, 4)),
+            sem((NX, 3)),
+            sem((NX, 3)),
+            sem((NX - 1, 2)),
+            sem((NX - 1, 2)),
         ],
         compiler_params=pltpu.CompilerParams(
-            collective_id=4, has_side_effects=True, vmem_limit_bytes=48 * 1024 * 1024
+            collective_id=3, has_side_effects=True, vmem_limit_bytes=58 * 1024 * 1024
         ),
-        name="collect",
-    )(part)
+        name="run_experts",
+    )(slots, source, up, down)
 
 
 def home_kernel(slots, weights, rows_in, hidden, out, sums, staged, landed, zs, zr):
@@ -951,15 +928,12 @@
     slot_token = jnp.where(token >= 0, token + first, -1).transpose(1, 0, 2)
     slot_weight = slab_all[:, :, 128 : 128 + capacity].transpose(1, 0, 2)
     groups, size = NY * NX, NZ * capacity
-    rows = dispatch(
-        slot_token.reshape(NY, NX, size, 1), spread.reshape(NZ * row_count, quarter)
-    )
-    value = run_expert(
-        rows.reshape(quarters, groups, size, quarter),
+    returned = run_experts(
+        slot_token.reshape(NY, NX, size, 1),
+        spread.reshape(NZ * row_count, quarter),
         w_gate_up[0].transpose(1, 2, 0),
         w_down[0],
     )
-    returned = collect(value.reshape(quarters, NY, NX, size, quarter))
     layer_output = bring_home(
         slot_token.reshape(1, groups * size),
         slot_weight.reshape(1, groups * size),

time: 299 us -> 261 us (0.87); the launches traced: 298 us -> 256 us
  Pallas kernels: 278 us -> 236 us
    pallas_call x3 -> x1, Pallas kernels: 133 us -> 92.6 us  [run_experts(): pl.pallas_call(expert_kernel, out_shape=jax.ShapeDtypeStruct((NY, NX) + p...]
where the time goes in v4:
time: 261 us; the launch traced here: 256 us
  Pallas kernels  236 us (90%)
  local copies, waits for them, and re-layouts  17.3 us (7%)
    pallas_call x1, Pallas kernels, run_experts(): pl.pallas_call(expert_kernel, out_shape=jax.ShapeDtypeStruct((NY, NX) + p...  92.6 us
    pallas_call x1, Pallas kernels, norm_and_spread(): pl.pallas_call(functools.partial(norm_kernel, model_width), out_shape=(ja...  47.6 us
    pallas_call x1, Pallas kernels, front(): pl.pallas_call(functools.partial(front_kernel, scale), out_shape=(jax.Sha...  38.3 us
    pallas_call x1, Pallas kernels, attend(): pl.pallas_call(functools.partial(attend_kernel, cache_rows), grid=(seqs,...  34.3 us
    pallas_call x1, Pallas kernels, bring_home(): pl.pallas_call(home_kernel, out_shape=jax.ShapeDtypeStruct(hidden.shape,...  21.7 us
    unnamed x18, local copies, waits for them, and re-layouts  9.85 us

profile of v4, /device:TPU:40, one launch (start us, length us, event | category | flops | bytes accessed | tf_op | source)
XLA Modules:
  0.0 256.3 jit_solution(14941662806128950896)
XLA Ops:
  0.6 0.7 pad_add_fusion.place
  1.4 0.7 add_convert_fusion
  2.2 0.8 dynamic_slice.3
  3.0 0.7 copy.25
  3.7 0.7 reshape.75.routed
  4.3 0.7 copy.26
  5.7 0.8 reshape.74.gain
  6.6 1.9 route.1
  8.5 0.9 copy.36
  9.4 1.0 copy.23
  10.4 1.8 copy-done.1
  12.2 1.1 copy-done.4
  13.3 0.8 copy-done.7
  14.2 38.3 %front.1 = (bf16[2,64,128]{2,1,0:T(8,128)(2,1)S(1)}, bf16[16,2,256,128]{3,2,1,0:T(8,128)(2,1)S(1)}, bf16[4,2,64,512]{3,2,1,0:T(8,128)(2,1)S(1)}, f32[8,8,256]{2,1,0:T(8,128)S(1)}) custom-call(bf16[128,720]{1,0:T(8,128)(2,1)S(1)} %bitcast.32, f32[4,1,720]{2,1,0:T(1,128)S(1)} %reshape.74.gain, bf16[2880,512]{1,0:T(8,128)(2,1)S(1)} %copy-done.1, ...), custom_call_target="tpu_custom_call" | custom-call | tf_op jit(solution)/shard_map/front/pallas_call | solution.py:220
  52.5 34.3 %attend.1 = (bf16[4,2,64,512]{3,2,1,0:T(8,128)(2,1)S(1)}, f32[4,2,8,512]{3,2,1,0:T(8,128)S(1)}) custom-call(s32[3]{0:T(128)S(1)} %pad_add_fusion.place, bf16[4,2,64,512]{3,2,1,0:T(8,128)(2,1)S(1)} %get-tuple-element.11.q_ref, bf16[16,2,256,128]{3,2,1,0:T(8,128)(2,1)S(1)} %get-tuple-element.12.kv_ref), custom_call_target="tpu_custom_call" | custom-call | tf_op jit(solution)/shard_map/attend/pallas_call | solution.py:325
  86.8 0.8 copy-done.5
  88.6 1.1 reshape.86.slots
  89.7 1.0 copy-done.6
  90.7 47.6 %norm_and_spread.1 = (bf16[128,720]{1,0:T(8,128)(2,1)S(1)}, bf16[8,128,720]{2,1,0:T(8,128)(2,1)S(1)}) custom-call(bf16[4,2,64,512]{3,2,1,0:T(8,128)(2,1)S(1)} %copy-done.6, f32[4,2,8,512]{3,2,1,0:T(8,128)S(1)} %get-tuple-element.14.stat, bf16[2880,512]{1,0:T(8,128)(2,1)S(1)} %bitcast.31, bf16[128,720]{1,0:T(8,128)(2,1)S(1)} %bitcast.33, ...), custom_call_target="tpu_custom_call" | custom-call | tf_op jit(solution)/shard_map/norm_and_spread/pallas_call | solution.py:480
  138.3 1.1 copy-done.3
  139.5 92.6 %run_experts.1 = bf16[2,4,160,720]{3,2,1,0:T(8,128)(2,1)} custom-call(s32[2,4,160,1]{3,2,1,0:T(8,128)} %reshape.86.slots, bf16[1024,720]{1,0:T(8,128)(2,1)} %bitcast.34, bf16[2,360,2880]{2,1,0:T(8,128)(2,1)} %bitcast.40, bf16[360,2880]{1,0:T(8,128)(2,1)} %bitcast.41), custom_call_target="tpu_custom_call" | custom-call | tf_op jit(solution)/shard_map/run_experts/pallas_call | solution.py:697
  232.1 1.5 copy-done
  233.6 21.7 %bring_home.1 = bf16[128,720]{1,0:T(8,128)(2,1)S(1)} custom-call(s32[1,1280]{1,0:T(1,128)S(1)} %reshape.78.slots, f32[1,1280]{1,0:T(1,128)S(1)} %reshape.79.weights, bf16[1280,720]{1,0:T(8,128)(2,1)S(1)} %bitcast.30, bf16[128,720]{1,0:T(8,128)(2,1)S(1)} %get-tuple-element.16.hidden), custom_call_target="tpu_custom_call" | custom-call | tf_op jit(solution)/shard_map/bring_home/pallas_call | solution.py:801
  255.4 0.9 copy.35
  (23 shorter events, 1.9 us)
Async XLA Ops:
  10.4 1.8 copy-start.1
  12.2 1.1 copy-start.4
  13.3 0.8 copy-start.7
  52.5 37.2 %copy-start.2 = (bf16[512,2880]{0,1:T(8,128)(2,1)S(1)}, bf16[512,2880]{0,1:T(8,128)(2,1)}, u32[]{:S(2)}) copy-start(bf16[512,2880]{0,1:T(8,128)(2,1)} %param.16) | copy-start | bytes 8847364
  86.8 0.8 copy-start.5
  89.7 1.0 copy-start.6
  138.3 1.1 copy-start.3
  232.1 1.5 copy-start
